TPU v7x, 128 devices: a whole 4x4x4 slice. The times are simulated.
128 devices in a mesh: ctx: 8 (over z, core), ch: 16 (over y, x).
Axes of the slice: x: 4, y: 4, z: 4, core: 2. Of those that a mesh axis runs over, the one named last changes fastest.
Arguments:
- x_owned: bfloat16 [8192, 8192], P('ctx', 'ch'), may hold values from -40 to 40
- live_blocks: int32 [8], replicated, may hold values from 0 to 8, as said below
- seq_lengths: int32 [3], replicated, may hold values from 1 to 2048, as said below
- norm_gain: float32 [8192], replicated, may hold values from 0.5 to 1.5
- w_in: bfloat16 [3, 8192, 4096], P(None, None, 'ch'), may hold values from -0.0625 to 0.0625
- w_short: float32 [3, 3, 4096], P(None, None, 'ch'), may hold values from -2.5 to 2.5
- decay_rates: float32 [16, 4096], P(None, 'ch'), may hold values from 4.8828125e-06 to 0.03
- residues: float32 [16, 4096], P(None, 'ch'), may hold values from -1.5 to 1.5
- skip_gain: float32 [4096], P('ch'), may hold values from 0.5 to 1.5
- w_out: bfloat16 [4096, 8192], P('ch'), may hold values from -0.09375 to 0.09375
Outputs:
- out: bfloat16 [8192, 4096], P('ch', 'ctx')
Inputs may be any that keep to these rules, and one draw needn't show every extreme that they name: `live_blocks`: the counts sum to 32. The live blocks of buffers 0 .. s - 1 number s * 4 + e with e between -2 and 2, and both ends occur. Rows of a buffer past its live blocks are never read. `seq_lengths`: the lengths sum to 4096.
All inputs are finite; a program needn't handle non-finite values.
Results may differ from a plain program's by a relative error of at most 0.02.
Values may be sent and summed in bfloat16 or wider, within the bound.
A program may use at most 128 MiB of HBM per device.

v0:
```python
import jax
import jax.numpy as jnp
from jax import lax
from jax.sharding import PartitionSpec as P

D = 8192
TAPS = 3
BLOCK = 128
SEQS = 3


EPS = 1e-06
HIGHEST = lax.Precision.HIGHEST


def segment_of(seq_lengths, positions):
    ends_at = jnp.cumsum(seq_lengths)
    inside = jnp.sum((positions[:, None] >= ends_at[None, :]).astype(jnp.int32), axis=1)
    return jnp.where(positions < 0, -1, inside)


def link_states(earlier, later):
    return (earlier[0] * later[0], later[0] * earlier[1] + later[1])


def project(x_rows, norm_gain, w_in):
    whole_rows = lax.all_gather(x_rows, "ch", axis=1, tiled=True)
    widened = whole_rows.astype(jnp.float32)
    row_scale = lax.rsqrt(jnp.sum(widened * widened, axis=1, keepdims=True) / D + EPS)
    normed = (widened * row_scale * norm_gain[None, :]).astype(jnp.bfloat16)
    summed = jnp.einsum("bdc,td->bct", w_in, normed, preferred_element_type=jnp.float32)
    return summed.astype(jnp.bfloat16)


def to_channels(projected):
    ctx_count = lax.axis_size("ctx")
    branches, width_here, row_count = projected.shape
    grouped = projected.reshape(branches, ctx_count, width_here // ctx_count, row_count)
    moved = lax.all_to_all(grouped, "ctx", split_axis=1, concat_axis=3, tiled=True)
    return moved.reshape(branches, width_here // ctx_count, ctx_count * row_count)


def to_tokens(gated_out):
    ctx_count = lax.axis_size("ctx")
    group_width, length = gated_out.shape
    moved = lax.all_to_all(
        gated_out.reshape(group_width, ctx_count, length // ctx_count),
        "ctx",
        split_axis=1,
        concat_axis=0,
        tiled=True,
    )
    return moved.reshape(ctx_count * group_width, length // ctx_count)


def short_mix(widened, segment_all, tap_weights):
    length = widened.shape[2] - (TAPS - 1)
    current = segment_all[TAPS - 1 :]
    mixed = jnp.zeros((widened.shape[0], widened.shape[1], length), jnp.float32)
    for tap_index in range(TAPS):
        begin_at = TAPS - 1 - tap_index
        same_seq = (segment_all[begin_at : begin_at + length] == current).astype(jnp.float32)
        mixed = (
            mixed
            + tap_weights[tap_index][:, :, None]
            * widened[:, :, begin_at : begin_at + length]
            * same_seq[None, None, :]
        )
    return (mixed[0], mixed[1] * mixed[2])


def filter_terms(decay_rates, residues, block_size):
    lag_steps = jnp.arange(block_size, dtype=jnp.float32)
    mode_weight = residues * jnp.sqrt(-jnp.expm1(-2.0 * decay_rates))
    rise_weight = mode_weight[:, :, None] * jnp.exp(-decay_rates[:, :, None] * (lag_steps + 1.0))
    fall_decay = jnp.exp(-decay_rates[:, :, None] * (block_size - 1.0 - lag_steps))
    whole_decay = jnp.exp(-decay_rates * block_size)
    lag_gap = lag_steps[:, None] - lag_steps[None, :]
    causal = (lag_gap >= 0).astype(jnp.float32)
    clipped = jnp.maximum(lag_gap, 0.0)
    toeplitz = jnp.zeros((decay_rates.shape[1], block_size, block_size), jnp.float32)
    for mode_index in range(decay_rates.shape[0]):
        toeplitz = toeplitz + mode_weight[mode_index][:, None, None] * jnp.exp(
            -decay_rates[mode_index][:, None, None] * clipped[None]
        )
    return (rise_weight, fall_decay, whole_decay, toeplitz * causal[None])


def local_pass(gated_input, segment, segment_before, filter_set):
    rise_weight, fall_decay, whole_decay, toeplitz = filter_set
    channels, length = gated_input.shape
    block_size = toeplitz.shape[1]
    block_count = length // block_size
    input_blocks = gated_input.reshape(channels, block_count, block_size)
    segment_blocks = segment.reshape(block_count, block_size)
    label_ids = jnp.arange(SEQS, dtype=jnp.int32)
    membership = (segment_blocks[None] == label_ids[:, None, None]).astype(jnp.float32)
    inner_sum = jnp.einsum(
        "cij,scbj->scbi", toeplitz, membership[:, None] * input_blocks[None], precision=HIGHEST
    )
    near_part = jnp.sum(membership[:, None] * inner_sum, axis=0)
    last_seg = segment_blocks[:, block_size - 1]
    prev_last = jnp.concatenate([jnp.reshape(segment_before, (1,)), last_seg[:-1]])
    keep_carry = (last_seg == prev_last).astype(jnp.float32)
    tail_mask = (segment_blocks == last_seg[:, None]).astype(jnp.float32)
    end_states = jnp.einsum(
        "mcj,cbj->mcb", fall_decay, input_blocks * tail_mask[None], precision=HIGHEST
    )
    block_steps = whole_decay[:, :, None] * keep_carry[None, None, :]
    factor_run, state_run = lax.associative_scan(link_states, (block_steps, end_states), axis=2)
    before_factor = jnp.concatenate(
        [jnp.ones_like(factor_run[:, :, :1]), factor_run[:, :, :-1]], axis=2
    )
    before_state = jnp.concatenate(
        [jnp.zeros_like(state_run[:, :, :1]), state_run[:, :, :-1]], axis=2
    )
    carry_mask = (segment_blocks == prev_last[:, None]).astype(jnp.float32)
    cross_part = jnp.einsum("mci,mcb->cbi", rise_weight, before_state, precision=HIGHEST)
    near_part = (near_part + cross_part * carry_mask[None]).reshape(channels, length)
    summary = (factor_run[:, :, block_count - 1], state_run[:, :, block_count - 1])
    return (near_part, before_factor, carry_mask, summary)


def channel_filter(spread, seq_lengths, w_short, decay_rates, residues, skip_gain):
    group_width = spread.shape[1]
    first_channel = lax.axis_index("ctx") * group_width
    tap_weights = lax.dynamic_slice_in_dim(w_short, first_channel, group_width, 2)
    rate_part = lax.dynamic_slice_in_dim(decay_rates, first_channel, group_width, 1)
    residue_part = lax.dynamic_slice_in_dim(residues, first_channel, group_width, 1)
    skip_part = lax.dynamic_slice_in_dim(skip_gain, first_channel, group_width, 0)
    length = spread.shape[2]
    segment_all = segment_of(seq_lengths, jnp.arange(-(TAPS - 1), length, dtype=jnp.int32))
    widened = jnp.pad(spread, ((0, 0), (0, 0), (TAPS - 1, 0))).astype(jnp.float32)
    query_part, gated_input = short_mix(widened, segment_all, tap_weights)
    filter_set = filter_terms(rate_part, residue_part, BLOCK)
    passed = local_pass(gated_input, segment_all[TAPS - 1 :], segment_all[TAPS - 2], filter_set)
    return (query_part * (passed[0] + skip_part[:, None] * gated_input)).astype(jnp.bfloat16)


def body(
    x_owned,
    live_blocks,
    seq_lengths,
    norm_gain,
    w_in,
    w_short,
    decay_rates,
    residues,
    skip_gain,
    w_out,
):
    ctx_count = lax.axis_size("ctx")
    per_device = x_owned.shape[0] // (2 * BLOCK)
    ends_at = jnp.cumsum(live_blocks)
    starts_at = ends_at - live_blocks
    projected = project(x_owned, norm_gain, w_in)
    spread = to_channels(projected)
    capacity = 2 * per_device
    block_index = jnp.arange(ctx_count * per_device, dtype=jnp.int32)
    owner_index = jnp.sum((block_index[:, None] >= ends_at[None, :]).astype(jnp.int32), axis=1)
    owner_onehot = (owner_index[:, None] == jnp.arange(ctx_count, dtype=jnp.int32)[None, :]).astype(
        jnp.int32
    )
    slot_index = block_index - jnp.sum(owner_onehot * starts_at[None, :], axis=1)
    source = owner_index * capacity + slot_index
    pieces = spread.reshape(3, spread.shape[1], ctx_count * capacity, BLOCK)
    ordered = jnp.take(pieces, source, axis=2).reshape(
        3, spread.shape[1], ctx_count * per_device * BLOCK
    )
    tokens_out = to_tokens(
        channel_filter(ordered, seq_lengths, w_short, decay_rates, residues, skip_gain)
    )
    return lax.psum_scatter(
        jnp.einsum("cd,ct->dt", w_out, tokens_out, preferred_element_type=jnp.float32).astype(
            jnp.bfloat16
        ),
        "ch",
        scatter_dimension=0,
        tiled=True,
    )


def solution(mesh):
    return jax.shard_map(
        body,
        mesh=mesh,
        in_specs=(
            P("ctx", "ch"),
            P(),
            P(),
            P(),
            P(None, None, "ch"),
            P(None, None, "ch"),
            P(None, "ch"),
            P(None, "ch"),
            P("ch"),
            P("ch", None),
        ),
        out_specs=P("ch", "ctx"),
        check_vma=False,
    )
```

profile of v0, /device:TPU:0, one launch (start us, length us, event | category | flops | bytes accessed | tf_op | source)
XLA Modules:
  0.0 389.8 jit_solution(3215478067377386300)
XLA Ops:
  13.9 1.7 fusion.151
  16.9 115.9 %all-gather.2.cloned.1.call-done = bf16[1024,8192]{1,0:T(8,128)(2,1)} async-done(((bf16[1024,512]{1,0:T(8,128)(2,1)}), bf16[1024,8192]{1,0:T(8,128)(2,1)}) %all-gather.2.cloned.1.call-update) | async-done | bytes 16777232 | tf_op jit(solution)/shard_map/all_gather | solution.py:27
  132.9 7.2 %fusion = f32[1024]{0:T(1024)S(1)} fusion(bf16[1024,8192]{1,0:T(8,128)(2,1)} %all-gather.2.cloned.1.call-done), kind=kLoop, calls=%fused_computation.3 | loop fusion | flops 25164800 | bytes 16781312 | tf_op jit(solution)/shard_map/reduce_sum | solution.py:29
  140.1 27.0 %fusion.75 = bf16[1024,3,256]{0,2,1:T(8,128)(2,1)S(1)} fusion(bf16[3,8192,256]{2,1,0:T(8,128)(2,1)} %param.14, bf16[1024,8192]{1,0:T(8,128)(2,1)} %all-gather.2.cloned.1.call-done, f32[8192]{0:T(1024)S(1)} %copy-done.45, f32[1024]{0:T(1024)S(1)} %add_rsqrt_fusion), kind=kOutput, calls=%fused_computation.78 | convolution fusion | flops 12919242752 | bytes 30969856 | tf_op jit(solution)/shard_map/bdc,td->bct/dot_general | solution.py:31
  168.5 4.6 %all-to-all-start = ((bf16[3,8,32,1024]{3,2,0,1:T(8,128)(2,1)}), bf16[3,8,32,1024]{3,2,0,1:T(8,128)(2,1)S(1)}, u32[]{:S(2)}, u32[]{:S(2)}) async-start(bf16[3,8,32,1024]{3,2,0,1:T(8,128)(2,1)} %copy.57), calls=%async_computation | async-start | bytes 3145728 | tf_op jit(solution)/shard_map/all_to_all | solution.py:39
  173.8 2.3 slice.312
  176.1 2.4 slice.308
  178.5 1.8 slice.307
  183.9 10.7 %all-to-all-done = bf16[3,8,32,1024]{3,2,0,1:T(8,128)(2,1)S(1)} async-done(((bf16[3,8,32,1024]{3,2,0,1:T(8,128)(2,1)}), bf16[3,8,32,1024]{3,2,0,1:T(8,128)(2,1)S(1)}, u32[]{:S(2)}, u32[]{:S(2)}) %all-to-all-start) | async-done | bytes 1572896 | tf_op jit(solution)/shard_map/all_to_all | solution.py:39
  201.9 2.4 slice.340
  204.3 1.9 slice.310
  206.1 2.4 slice.309
  211.8 1.9 slice.313
  213.7 1.9 slice.338
  215.6 1.9 slice.316
  217.5 1.9 slice.315
  221.2 1.7 slice.320
  223.0 1.6 slice.319
  226.2 1.7 slice.322
  243.4 2.3 pad.40
  245.6 2.3 pad.39
  249.3 2.4 pad.41
  251.7 2.4 pad.42
  255.4 2.7 pad.43
  258.0 2.7 pad.44
  261.4 3.2 pad.59
  264.6 3.2 pad.77
  268.2 10.3 %multiply_reduce_fusion = f32[32,32,128]{2,1,0:T(8,128)S(1)} fusion(f32[128,128]{1,0:T(8,128)S(1)} %copy-done.5, f32[32]{0:T(128)S(1)} %copy-done.12, f32[32]{0:T(128)S(1)} %copy-done.28, f32[32]{0:T(128)S(1)} %copy-done.13, f32[32]{0:T(128)S(1)} %copy-done.29, f32[32]{0:T(128)S(1)} %copy-done.14, f32[32]{0:T(128)S(1)} %copy-done.30, f32[32]{0:T(128)S(1)} %copy-done.15, ...), kind=kOutput, calls=%fused_computation.86 | convolution fusion | flops 630194176 | bytes 1232896 | tf_op jit(solution)/shard_map/cij,scbj->scbi/dot_general | solution.py:98
  280.5 9.9 %all_to_all.30 = bf16[32,8,512]{2,0,1:T(8,128)(2,1)S(1)} all-to-all(bf16[32,8,512]{2,0,1:T(8,128)(2,1)S(1)} %copy.68), channel_id=1, replica_groups=mesh['ctx'=8,'ch'=16] {'ctx'}, dimensions={1} | all-to-all | bytes 524288 | tf_op jit(solution)/shard_map/all_to_all | solution.py:46
  290.4 7.8 %fusion.8 = bf16[8192,512]{0,1:T(8,128)(2,1)} fusion(bf16[256,512]{1,0:T(8,128)(2,1)S(1)} %bitcast.163, bf16[256,8192]{1,0:T(8,128)(2,1)} %param.19), kind=kOutput, calls=%fused_computation.11 | convolution fusion | flops 2151677952 | bytes 12845056 | tf_op jit(solution)/shard_map/cd,ct->dt/dot_general | solution.py:174
  298.3 82.6 %reduce-scatter.2.cloned.1.call-done = bf16[512,512]{0,1:T(8,128)(2,1)} async-done(((bf16[8192,512]{0,1:T(8,128)(2,1)}), bf16[512,512]{0,1:T(8,128)(2,1)}) %reduce-scatter.2.cloned.1.call-update) | async-done | bytes 524304 | tf_op jit(solution)/shard_map/reduce_scatter | solution.py:173
  380.9 2.0 copy.69
  (180 shorter events, 48.6 us)
Async XLA Ops:
  6.5 126.3 %all-gather.2.cloned.1.call-start = ((), (), s32[]{:S(2)}) async-start(), calls=%async_computation.3 | async-start | bytes 17825792 | tf_op jit(solution)/shard_map/all_gather | solution.py:27
  16.9 123.1 %copy-start.45 = (f32[8192]{0:T(1024)S(1)}, f32[8192]{0:T(1024)}, u32[]{:S(2)}) copy-start(f32[8192]{0:T(1024)} %param.13) | copy-start | bytes 98308
  168.5 11.8 %copy-start.46 = (f32[256]{0:T(256)S(1)}, f32[256]{0:T(256)}, u32[]{:S(2)}) copy-start(f32[256]{0:T(256)} %param.18) | copy-start | bytes 3076
  168.5 26.1 %all-to-all-start = ((bf16[3,8,32,1024]{3,2,0,1:T(8,128)(2,1)}), bf16[3,8,32,1024]{3,2,0,1:T(8,128)(2,1)S(1)}, u32[]{:S(2)}, u32[]{:S(2)}) async-start(bf16[3,8,32,1024]{3,2,0,1:T(8,128)(2,1)} %copy.57), calls=%async_computation | async-start | bytes 3145728 | tf_op jit(solution)/shard_map/all_to_all | solution.py:39
  173.0 207.9 %reduce-scatter.2.cloned.1.call-start = ((), (), s32[]{:S(2)}) async-start(), calls=%async_computation.4 | async-start | bytes 8912896 | tf_op jit(solution)/shard_map/reduce_scatter | solution.py:173
  200.3 8.2 %copy-start.3 = (f32[16,32,16]{2,0,1:T(8,128)S(1)}, f32[16,32,16]{2,0,1:T(8,128)}, u32[]{:S(2)}) copy-start(f32[16,32,16]{2,0,1:T(8,128)} %slice.312) | copy-start | bytes 98308
  200.3 8.2 %copy-start.4 = (f32[16,32,16]{2,0,1:T(8,128)S(1)}, f32[16,32,16]{2,0,1:T(8,128)}, u32[]{:S(2)}) copy-start(f32[16,32,16]{2,0,1:T(8,128)} %slice.308) | copy-start | bytes 98308
  260.8 7.0 %copy-start.5 = (f32[128,128]{1,0:T(8,128)S(1)}, f32[128,128]{1,0:T(8,128)}, u32[]{:S(2)}) copy-start(f32[128,128]{1,0:T(8,128)} %fusion.146) | copy-start | bytes 196612
  260.8 7.0 %copy-start.6 = (f32[128,128]{1,0:T(8,128)S(1)}, f32[128,128]{1,0:T(8,128)}, u32[]{:S(2)}) copy-start(f32[128,128]{1,0:T(8,128)} %fusion.145) | copy-start | bytes 196612
  260.9 7.0 %copy-start.11 = (f32[32]{0:T(128)S(1)}, f32[32]{0:T(128)}, u32[]{:S(2)}) copy-start(f32[32]{0:T(128)} %get-tuple-element.26) | copy-start | bytes 388
  260.9 7.0 %copy-start.12 = (f32[32]{0:T(128)S(1)}, f32[32]{0:T(128)}, u32[]{:S(2)}) copy-start(f32[32]{0:T(128)} %get-tuple-element.27) | copy-start | bytes 388
  260.9 7.0 %copy-start.13 = (f32[32]{0:T(128)S(1)}, f32[32]{0:T(128)}, u32[]{:S(2)}) copy-start(f32[32]{0:T(128)} %get-tuple-element.28) | copy-start | bytes 388
  260.9 7.0 %copy-start.14 = (f32[32]{0:T(128)S(1)}, f32[32]{0:T(128)}, u32[]{:S(2)}) copy-start(f32[32]{0:T(128)} %get-tuple-element.29) | copy-start | bytes 388
  260.9 7.0 %copy-start.15 = (f32[32]{0:T(128)S(1)}, f32[32]{0:T(128)}, u32[]{:S(2)}) copy-start(f32[32]{0:T(128)} %get-tuple-element.30) | copy-start | bytes 388
  260.9 7.0 %copy-start.16 = (f32[32]{0:T(128)S(1)}, f32[32]{0:T(128)}, u32[]{:S(2)}) copy-start(f32[32]{0:T(128)} %get-tuple-element.31) | copy-start | bytes 388
  260.9 7.0 %copy-start.17 = (f32[32]{0:T(128)S(1)}, f32[32]{0:T(128)}, u32[]{:S(2)}) copy-start(f32[32]{0:T(128)} %get-tuple-element.32) | copy-start | bytes 388
  260.9 7.0 %copy-start.18 = (f32[32]{0:T(128)S(1)}, f32[32]{0:T(128)}, u32[]{:S(2)}) copy-start(f32[32]{0:T(128)} %get-tuple-element.33) | copy-start | bytes 388
  260.9 7.0 %copy-start.19 = (f32[32]{0:T(128)S(1)}, f32[32]{0:T(128)}, u32[]{:S(2)}) copy-start(f32[32]{0:T(128)} %get-tuple-element.34) | copy-start | bytes 388
  260.9 7.0 %copy-start.20 = (f32[32]{0:T(128)S(1)}, f32[32]{0:T(128)}, u32[]{:S(2)}) copy-start(f32[32]{0:T(128)} %get-tuple-element.35) | copy-start | bytes 388
  261.0 7.0 %copy-start.21 = (f32[32]{0:T(128)S(1)}, f32[32]{0:T(128)}, u32[]{:S(2)}) copy-start(f32[32]{0:T(128)} %get-tuple-element.36) | copy-start | bytes 388
  261.0 7.0 %copy-start.22 = (f32[32]{0:T(128)S(1)}, f32[32]{0:T(128)}, u32[]{:S(2)}) copy-start(f32[32]{0:T(128)} %get-tuple-element.37) | copy-start | bytes 388
  261.0 7.0 %copy-start.23 = (f32[32]{0:T(128)S(1)}, f32[32]{0:T(128)}, u32[]{:S(2)}) copy-start(f32[32]{0:T(128)} %get-tuple-element.38) | copy-start | bytes 388
  261.0 7.0 %copy-start.24 = (f32[32]{0:T(128)S(1)}, f32[32]{0:T(128)}, u32[]{:S(2)}) copy-start(f32[32]{0:T(128)} %get-tuple-element.39) | copy-start | bytes 388
  261.0 7.0 %copy-start.25 = (f32[32]{0:T(128)S(1)}, f32[32]{0:T(128)}, u32[]{:S(2)}) copy-start(f32[32]{0:T(128)} %get-tuple-element.40) | copy-start | bytes 388
  261.0 7.0 %copy-start.26 = (f32[32]{0:T(128)S(1)}, f32[32]{0:T(128)}, u32[]{:S(2)}) copy-start(f32[32]{0:T(128)} %get-tuple-element.41) | copy-start | bytes 388
  261.0 7.0 %copy-start.27 = (f32[32]{0:T(128)S(1)}, f32[32]{0:T(128)}, u32[]{:S(2)}) copy-start(f32[32]{0:T(128)} %get-tuple-element.45) | copy-start | bytes 388
  261.0 7.0 %copy-start.28 = (f32[32]{0:T(128)S(1)}, f32[32]{0:T(128)}, u32[]{:S(2)}) copy-start(f32[32]{0:T(128)} %get-tuple-element.46) | copy-start | bytes 388
  261.0 7.0 %copy-start.29 = (f32[32]{0:T(128)S(1)}, f32[32]{0:T(128)}, u32[]{:S(2)}) copy-start(f32[32]{0:T(128)} %get-tuple-element.47) | copy-start | bytes 388
  261.0 7.0 %copy-start.30 = (f32[32]{0:T(128)S(1)}, f32[32]{0:T(128)}, u32[]{:S(2)}) copy-start(f32[32]{0:T(128)} %get-tuple-element.48) | copy-start | bytes 388
  261.1 7.0 %copy-start.31 = (f32[32]{0:T(128)S(1)}, f32[32]{0:T(128)}, u32[]{:S(2)}) copy-start(f32[32]{0:T(128)} %get-tuple-element.49) | copy-start | bytes 388
  261.1 7.0 %copy-start.32 = (f32[32]{0:T(128)S(1)}, f32[32]{0:T(128)}, u32[]{:S(2)}) copy-start(f32[32]{0:T(128)} %get-tuple-element.50) | copy-start | bytes 388
  268.2 10.3 %copy-start.10 = (f32[128]{0:T(128)S(1)}, f32[128]{0:T(128)}, u32[]{:S(2)}) copy-start(f32[128]{0:T(128)} %iota_add_fusion.1) | copy-start | bytes 1540
  (18 other events, 90.7 us)
Sparse Core Ops, SparseCore 0:
  9.5 123.3 all-gather.1
  298.4 82.4 reduce-scatter.1
where the time goes:
time: 391 us; the launch traced here: 390 us
  waiting for transfers between devices  210 us (54%)
  local copies, waits for them, and re-layouts  75.8 us (19%)
  matrix products  47.4 us (12%)
  other arithmetic  27.5 us (7%)
  between operations  14.5 us (4%)
  blocking collectives  9.95 us (3%)
  starting transfers between devices  4.78 us (1%)
    all_gather x1, waiting for transfers between devices, project(): whole_rows = lax.all_gather(x_rows, 'ch', axis=1, tiled=True)  116 us
    reduce_scatter x1, waiting for transfers between devices, body(): lax.psum_scatter(jnp.einsum('cd,ct->dt', w_out, tokens_out, preferred_ele...  82.6 us
    slice x23, local copies, waits for them, and re-layouts, local_pass(): lax.associative_scan(link_states, (block_steps, end_states), axis=2)  38.2 us
    dot_general x1, matrix products, project(): jnp.einsum('bdc,td->bct', w_in, normed, preferred_element_type=jnp.float32)  27 us
    pad x6, local copies, waits for them, and re-layouts, local_pass(): lax.associative_scan(link_states, (block_steps, end_states), axis=2)  14.7 us
    all_to_all x1, waiting for transfers between devices, to_channels(): lax.all_to_all(grouped, 'ctx', split_axis=1, concat_axis=3, tiled=True)  10.7 us
    dot_general x1, matrix products, local_pass(): jnp.einsum('cij,scbj->scbi', toeplitz, membership[:, None] * input_blocks...  10.3 us
    all_to_all x1, blocking collectives, to_tokens(): lax.all_to_all(gated_out.reshape(group_width, ctx_count, length // ctx_co...  9.95 us
  transfers between devices with their start and end apart: 3, of which 3 were waited for; matrix products, arithmetic and copies ran while one was open for 5% of the time, Pallas kernels for 0%

commit v1 on v0

v1 whole, which is shorter than its diff:
```python
import functools

import jax
import jax.numpy as jnp
from jax import lax
from jax.experimental import pallas as pl
from jax.experimental.pallas import tpu as pltpu
from jax.sharding import PartitionSpec as P

EPS = 1e-06
TAPS = 3
BRANCHES = 3
SIDE = 4
LANES = 128
GROUPS = 8
MESH = pl.DeviceIdType.MESH


def remote(src, dst, send_sem, recv_sem, device):
    return pltpu.make_async_remote_copy(
        src_ref=src,
        dst_ref=dst,
        send_sem=send_sem,
        recv_sem=recv_sem,
        device_id=device,
        device_id_type=MESH,
    )


def each(lower, upper, step):
    def run(index, carry):
        step(index)
        return carry

    lax.fori_loop(lower, upper, run, 0)


def plane_gather(buf, send_sems, recv_sems, ctx, row, col, use):
    half = buf.shape[2]
    quarter = half // 2
    rows = (pl.ds(0, half), pl.ds(0, half), pl.ds(0, quarter), pl.ds(quarter, quarter))

    def place(h, first, second):
        x = lax.rem(col + (1 - h) * first + h * second + 2 * SIDE, SIDE)
        y = lax.rem(row + (1 - h) * second + h * first + 2 * SIDE, SIDE)
        return y * SIDE + x

    def offset(ring):
        k = ring - 1
        return k + k // 2 - 2 * (k // 3)

    def piece(ring, h, along):
        if isinstance(ring, int) and ring == 0:
            return place(h, along, 0)
        return place(h, offset(ring), along)

    def neighbour(ring, h, along):
        if isinstance(ring, int) and ring == 0:
            return (ctx, place(h, along, 0))
        return (ctx, place(h, 0, along))

    def copy(ring, h, kind, along):
        part = buf.at[piece(ring, h, along), h, rows[kind]]
        return remote(
            part,
            part,
            send_sems.at[ring, h, kind],
            recv_sems.at[ring, h, kind],
            neighbour(ring, h, 1 - 2 * (kind % 2)),
        )

    def send(ring, h):
        copy(ring, h, 0, 0).start()
        copy(ring, h, 1, 0).start()

    def forward(ring, h):
        copy(ring, h, 0, -1).wait_recv()
        copy(ring, h, 2, -1).start()
        copy(ring, h, 1, 1).wait_recv()
        copy(ring, h, 3, 1).start()

    def finish(ring, h):
        copy(ring, h, 2, 2).wait_recv()
        copy(ring, h, 3, 2).wait_recv()

    def open_rings(h):
        send(0, h)
        send(1, h)

    def grow(h):
        forward(0, h)
        send(2, h)
        send(3, h)

    def close_first(h):
        finish(0, h)
        send(4, h)

    each(0, 2, open_rings)
    each(0, 2, lambda h: use(h, place(h, 0, 0)))
    each(0, 2, grow)
    each(0, 4, lambda i: use(i // 2, piece(0, i // 2, 2 * (i % 2) - 1)))
    each(0, 2, close_first)
    each(0, 2, lambda h: use(h, piece(0, h, 2)))

    def pass_on(ring):
        each(0, 2, lambda h: forward(ring, h))
        each(0, 4, lambda i: use(i // 2, piece(ring, i // 2, 2 * (i % 2) - 1)))

    def take_last(ring):
        each(0, 2, lambda h: finish(ring, h))
        each(0, 2, lambda h: use(h, piece(ring, h, 2)))

    each(1, SIDE + 1, pass_on)
    each(1, SIDE + 1, take_last)

    def drain(index):
        h = index % 2
        for kind in range(4):
            copy(0, h, kind, 0).wait_send()
        each(1, SIDE + 1, lambda ring: drain_ring(ring, h))

    def drain_ring(ring, h):
        for kind in range(4):
            copy(ring, h, kind, 0).wait_send()

    each(0, 2, drain)


def kernel(
    dims,
    live_ref,
    lengths_ref,
    gain_ref,
    taps_ref,
    rates_ref,
    weight_ref,
    skip_ref,
    x_hbm,
    w_in_hbm,
    w_out_hbm,
    out_ref,
    comb,
    last_blocks,
    x_all,
    w_in,
    sums,
    squares,
    proj,
    query,
    gated,
    ends,
    starts,
    edge,
    mixed,
    g_all,
    out_sum,
    w_stage,
    w_half,
    w_mine,
    local_sems,
    shift_sems,
    split_sems,
    deep_sems,
    relay_sems,
    edge_sems,
    x_send,
    x_recv,
    g_send,
    g_recv,
):
    ctx_count, tokens, block, width = dims
    ctx = lax.axis_index("ctx")
    ch = lax.axis_index("ch")
    row = ch // SIDE
    col = lax.rem(ch, SIDE)
    partner = ctx + 1 - 2 * lax.rem(ctx, 2)
    depth_count = ctx_count // 2
    capacity = x_hbm.shape[0] // block
    own_blocks = tokens // block
    features = x_hbm.shape[1]
    part_rows = w_out_hbm.shape[0] // ctx_count
    half = tokens // 2
    modes = rates_ref.shape[0]
    tiles = rates_ref.shape[1] // LANES
    run = tokens // GROUPS

    x_in = pltpu.make_async_copy(x_hbm, comb.at[pl.ds(0, capacity * block)], local_sems.at[0])
    x_in.start()

    def w_part(other, target, sem):
        return pltpu.make_async_copy(
            w_out_hbm.at[
                pl.ds(pl.multiple_of(ctx * part_rows, part_rows), part_rows),
                pl.ds(pl.multiple_of(other * features, features), features),
            ],
            target,
            sem,
        )

    for x in range(SIDE):
        for y in range(SIDE):
            w_part(y * SIDE + x, w_stage.at[x, y], local_sems.at[2 + x * SIDE + y]).start()
    w_load = pltpu.make_async_copy(w_in_hbm, w_in, local_sems.at[1])
    w_load.start()

    barrier = pltpu.get_barrier_semaphore()
    for step in range(1, SIDE):
        pl.semaphore_signal(
            barrier, inc=1, device_id=(ctx, row * SIDE + lax.rem(col + step, SIDE)), device_id_type=MESH
        )
        pl.semaphore_signal(
            barrier, inc=1, device_id=(ctx, lax.rem(row + step, SIDE) * SIDE + col), device_id_type=MESH
        )
    for step in range(1, ctx_count):
        pl.semaphore_signal(
            barrier, inc=1, device_id=(lax.rem(ctx + step, ctx_count), ch), device_id_type=MESH
        )
    sums[...] = jnp.zeros_like(sums)
    squares[...] = jnp.zeros_like(squares)
    out_sum[...] = jnp.zeros_like(out_sum)
    x_in.wait()

    before = jnp.int32(0)
    for owner in range(ctx_count):
        before = before + jnp.where(owner < ctx, live_ref[owner], 0)
    here = live_ref[ctx]
    left_live = live_ref[lax.rem(ctx + ctx_count - 1, ctx_count)]
    first_sent = jnp.maximum(here - 2, 0)
    def pick(which, options):
        value = comb[pl.ds(options[0] * block, block), :]
        for option in options[1:]:
            value = jnp.where(which == option, comb[pl.ds(option * block, block), :], value)
        return value

    for i in range(2):
        last_blocks[pl.ds(i * block, block), :] = pick(first_sent + i, list(range(i, capacity - 1 + i)))
    pl.semaphore_wait(barrier, 2 * (SIDE - 1) + ctx_count - 1)

    after = lax.rem(ctx + 1, ctx_count)
    ahead = lax.rem(ctx + ctx_count - 1, ctx_count)
    to_next = remote(
        last_blocks,
        comb.at[pl.ds(capacity * block, 2 * block)],
        shift_sems.at[0],
        shift_sems.at[1],
        (after, ch),
    )
    to_previous = remote(
        comb.at[pl.ds(0, 2 * block)],
        comb.at[pl.ds((capacity + 2) * block, 2 * block)],
        shift_sems.at[2],
        shift_sems.at[3],
        (ahead, ch),
    )
    to_next.start()
    to_previous.start()

    for x in range(SIDE):
        for y in range(SIDE):
            w_part(y * SIDE + x, w_stage.at[x, y], local_sems.at[2 + x * SIDE + y]).wait()

    def along_x(step):
        x = lax.rem(col + step, SIDE)
        return remote(
            w_stage.at[x],
            w_half.at[col],
            split_sems.at[0, 0, step],
            split_sems.at[0, 1, step],
            (ctx, row * SIDE + x),
        )

    def along_y(step):
        y = lax.rem(row + step, SIDE)
        return remote(
            w_half.at[:, y],
            w_mine.at[ctx, pl.ds(row * SIDE, SIDE)],
            split_sems.at[1, 0, step],
            split_sems.at[1, 1, step],
            (ctx, y * SIDE + col),
        )

    def over_depth(step):
        return remote(
            w_mine.at[ctx],
            w_mine.at[ctx],
            deep_sems.at[0, step],
            deep_sems.at[1, step],
            (lax.rem(ctx + 2 * step, ctx_count), ch),
        )

    def to_partner(step):
        held = lax.rem(ctx + 2 * step, ctx_count)
        return remote(
            w_mine.at[held],
            w_mine.at[held],
            relay_sems.at[0, step],
            relay_sems.at[1, step],
            (partner, ch),
        )

    for step in range(1, SIDE):
        along_x(step).start()
    own_x = pltpu.make_async_copy(w_stage.at[col], w_half.at[col], local_sems.at[0])
    own_x.start()
    own_x.wait()

    to_next.wait_recv()
    to_previous.wait_recv()
    first_wanted = ctx * own_blocks
    for i in range(own_blocks):
        wanted = first_wanted + i
        back = before - wanted
        from_left = capacity + left_live - back - jnp.maximum(left_live - 2, 0)
        from_right = capacity + 2 + wanted - before - here
        source = jnp.where(wanted < before, from_left, jnp.where(wanted >= before + here, from_right, wanted - before))
        nearby = list(range(max(i - 2, 0), min(i + 3, capacity))) + list(range(capacity, capacity + 4))
        x_all[ch, (2 * i) // own_blocks, pl.ds((i * block) % half, block), :] = pick(source, nearby)

    def project(h, g):
        wide = x_all[g, h].astype(jnp.float32)
        squared = wide * wide
        folded = squared[:, :LANES]
        for lane in range(1, features // LANES):
            folded = folded + squared[:, lane * LANES : (lane + 1) * LANES]
        at = pl.ds(pl.multiple_of(h * half, half), half)
        squares[at, :] = squares[at, :] + folded
        scaled = (wide * gain_ref[pl.ds(g, 1), :]).astype(jnp.bfloat16)
        deep = pl.ds(pl.multiple_of(g * features, features), features)
        for branch in range(BRANCHES):
            sums[branch, at, :] = sums[branch, at, :] + jnp.dot(
                scaled, w_in[branch, deep, :], preferred_element_type=jnp.float32
            )

    w_load.wait()
    for step in range(1, SIDE):
        along_x(step).wait_recv()
    for step in range(1, SIDE):
        along_y(step).start()
    own_y = pltpu.make_async_copy(w_half.at[:, row], w_mine.at[ctx, pl.ds(row * SIDE, SIDE)], local_sems.at[0])
    own_y.start()
    own_y.wait()
    for step in range(1, SIDE):
        along_y(step).wait_recv()
    for step in range(1, depth_count):
        over_depth(step).start()
    to_partner(0).start()
    plane_gather(x_all, x_send, x_recv, ctx, row, col, project)
    for step in range(1, depth_count):
        over_depth(depth_count - step).wait_recv()
        to_partner(step).start()

    def scale_rows(begin, count):
        total = jnp.sum(squares[pl.ds(begin, count), :], axis=1, keepdims=True)
        scale = lax.rsqrt(total / width + EPS)
        for branch in range(BRANCHES):
            for tile in range(tiles):
                proj[branch, tile, pl.ds(begin + 8, count), :] = (
                    sums[branch, pl.ds(begin, count), tile * LANES : (tile + 1) * LANES] * scale
                )

    scale_rows(tokens - run, run)
    halo = remote(
        proj.at[:, :, pl.ds(tokens, 8)],
        proj.at[:, :, pl.ds(0, 8)],
        shift_sems.at[4],
        shift_sems.at[5],
        (after, ch),
    )
    halo.start()
    each(0, GROUPS - 1, lambda i: scale_rows(pl.multiple_of(i * run, run), run))
    halo.wait_recv()

    cut_one = lengths_ref[0]
    cut_two = cut_one + lengths_ref[1]
    base = ctx * tokens
    group_start = base + run * lax.broadcasted_iota(jnp.int32, (GROUPS, LANES), 0)

    def keep_at(t):
        token = group_start + t
        begins = (token == 0) | (token == cut_one) | (token == cut_two)
        return jnp.where(begins, 0.0, 1.0).astype(jnp.float32)

    def unbroken(begin, count):
        cut = (begin == 0) | ((cut_one >= begin) & (cut_one < begin + count)) | ((cut_two >= begin) & (cut_two < begin + count))
        return jnp.where(cut, 0.0, 1.0).astype(jnp.float32)

    def spread_row(values):
        return jnp.broadcast_to(values, (GROUPS, LANES))

    for tile in range(tiles):
        lanes = pl.ds(tile * LANES, LANES)
        decays = [spread_row(jnp.exp(-rates_ref[pl.ds(m, 1), lanes])) for m in range(modes)]
        taps = [
            [spread_row(taps_ref[tap, pl.ds(branch, 1), lanes]) for branch in range(BRANCHES)]
            for tap in range(TAPS)
        ]

        def collect(t, carry, tile=tile, decays=decays, taps=taps):
            states, one_back, two_back, keep_before = carry
            keep = keep_at(t)
            far = keep * keep_before
            now = [proj[branch, tile, pl.ds(8 + t, GROUPS, stride=run), :] for branch in range(BRANCHES)]
            parts = [
                taps[0][branch] * now[branch]
                + taps[1][branch] * (keep * one_back[branch])
                + taps[2][branch] * (far * two_back[branch])
                for branch in range(BRANCHES)
            ]
            entered = parts[1] * parts[2]
            query[tile, t] = parts[0]
            gated[tile, t] = entered
            states = [decays[m] * (states[m] * keep) + entered for m in range(modes)]
            return (states, now, one_back, keep)

        first = [proj[branch, tile, pl.ds(7, GROUPS, stride=run), :] for branch in range(BRANCHES)]
        second = [proj[branch, tile, pl.ds(6, GROUPS, stride=run), :] for branch in range(BRANCHES)]
        zero = jnp.zeros((GROUPS, LANES), jnp.float32)
        done = lax.fori_loop(0, run, collect, ([zero] * modes, first, second, keep_at(-1)))
        for m in range(modes):
            ends[tile, pl.ds(m * GROUPS, GROUPS), :] = done[0][m]

    run_decay = [jnp.exp(-run * rates_ref[:, pl.ds(tile * LANES, LANES)]) for tile in range(tiles)]
    all_decay = [jnp.exp(-tokens * rates_ref[:, pl.ds(tile * LANES, LANES)]) for tile in range(tiles)]
    unbroken_run = [unbroken(base + run * i, run) for i in range(GROUPS)]

    for tile in range(tiles):
        state = jnp.zeros((modes, LANES), jnp.float32)
        for i in range(GROUPS):
            state = ends[tile, pl.ds(i, modes, stride=GROUPS), :] + (unbroken_run[i] * run_decay[tile]) * state
        edge[ctx, tile] = state

    def edge_to(step):
        return remote(
            edge.at[ctx],
            edge.at[ctx],
            edge_sems.at[0, step],
            edge_sems.at[1, step],
            (lax.rem(ctx + step, ctx_count), ch),
        )

    for step in range(1, ctx_count):
        edge_to(step).start()
    for step in range(1, ctx_count):
        edge_to(step).wait_recv()

    for tile in range(tiles):
        state = jnp.zeros((modes, LANES), jnp.float32)
        for device in range(ctx_count):
            moved = edge[device, tile] + (unbroken(jnp.int32(device * tokens), tokens) * all_decay[tile]) * state
            state = jnp.where(device < ctx, moved, state)
        for i in range(GROUPS):
            starts[tile, pl.ds(i, modes, stride=GROUPS), :] = state
            if i < GROUPS - 1:
                state = ends[tile, pl.ds(i, modes, stride=GROUPS), :] + (unbroken_run[i] * run_decay[tile]) * state

    for tile in range(tiles):
        lanes = pl.ds(tile * LANES, LANES)
        decays = [spread_row(jnp.exp(-rates_ref[pl.ds(m, 1), lanes])) for m in range(modes)]
        weights = [spread_row(weight_ref[pl.ds(m, 1), lanes]) for m in range(modes)]
        direct = spread_row(skip_ref[:, lanes])

        def filtered(t, states, tile=tile, decays=decays, weights=weights, direct=direct):
            keep = keep_at(t)
            entered = gated[tile, t]
            states = [decays[m] * (states[m] * keep) + entered for m in range(modes)]
            terms = [weights[m] * states[m] for m in range(modes)] + [direct * entered]
            while len(terms) > 1:
                terms = [
                    terms[k] + terms[k + 1] if k + 1 < len(terms) else terms[k]
                    for k in range(0, len(terms), 2)
                ]
            mixed[tile, pl.ds(t, GROUPS, stride=run), :] = query[tile, t] * terms[0]
            return states

        lax.fori_loop(
            0, run, filtered, [starts[tile, pl.ds(m * GROUPS, GROUPS), :] for m in range(modes)]
        )
        for h in range(2):
            g_all[ch, h, :, lanes] = mixed[tile, pl.ds(h * half, half), :].astype(jnp.bfloat16)

    for step in range(1, depth_count):
        to_partner(depth_count - step).wait_recv()
    to_partner(0).wait_recv()

    def multiply_out(h, g):
        weights = w_mine[:, g].reshape(ctx_count * part_rows, features)
        out_sum[h] = out_sum[h] + jnp.dot(g_all[g, h], weights, preferred_element_type=jnp.float32)

    plane_gather(g_all, g_send, g_recv, ctx, row, col, multiply_out)
    for h in range(2):
        out_ref[:, pl.ds(h * half, half)] = jnp.transpose(out_sum[h]).astype(jnp.bfloat16)

    to_next.wait_send()
    to_previous.wait_send()
    halo.wait_send()
    for step in range(1, SIDE):
        along_x(step).wait_send()
        along_y(step).wait_send()
    for step in range(1, depth_count):
        over_depth(step).wait_send()
    for step in range(depth_count):
        to_partner(step).wait_send()
    for step in range(1, ctx_count):
        edge_to(step).wait_send()


def body(
    x_owned,
    live_blocks,
    seq_lengths,
    norm_gain,
    w_in,
    w_short,
    decay_rates,
    residues,
    skip_gain,
    w_out,
):
    ctx_count = lax.axis_size("ctx")
    ch_count = lax.axis_size("ch")
    width = norm_gain.shape[0]
    features = x_owned.shape[1]
    tokens = x_owned.shape[0] // 2
    block = tokens // 4
    half = tokens // 2
    run = tokens // GROUPS
    modes, channels = decay_rates.shape
    tiles = channels // LANES
    part_rows = channels // ctx_count
    mode_weight = residues * jnp.sqrt(-jnp.expm1(-2.0 * decay_rates))
    bf16, f32 = jnp.bfloat16, jnp.float32
    smem = pl.BlockSpec(memory_space=pltpu.SMEM)
    vmem = pl.BlockSpec(memory_space=pltpu.VMEM)
    anywhere = pl.BlockSpec(memory_space=pl.ANY)
    dma = pltpu.SemaphoreType.DMA
    flops = 2 * tokens * width * BRANCHES * channels + 2 * tokens * features * ch_count * channels
    return pl.pallas_call(
        functools.partial(kernel, (ctx_count, tokens, block, width)),
        out_shape=jax.ShapeDtypeStruct((features, tokens), bf16),
        in_specs=[smem, smem, vmem, vmem, vmem, vmem, vmem, anywhere, anywhere, anywhere],
        out_specs=vmem,
        scratch_shapes=[
            pltpu.VMEM((x_owned.shape[0] + 4 * block, features), bf16),
            pltpu.VMEM((2 * block, features), bf16),
            pltpu.VMEM((ch_count, 2, half, features), bf16),
            pltpu.VMEM((BRANCHES, width, channels), bf16),
            pltpu.VMEM((BRANCHES, tokens, channels), f32),
            pltpu.VMEM((tokens, LANES), f32),
            pltpu.VMEM((BRANCHES, tiles, tokens + 8, LANES), f32),
            pltpu.VMEM((tiles, run, GROUPS, LANES), f32),
            pltpu.VMEM((tiles, run, GROUPS, LANES), f32),
            pltpu.VMEM((tiles, modes * GROUPS, LANES), f32),
            pltpu.VMEM((tiles, modes * GROUPS, LANES), f32),
            pltpu.VMEM((ctx_count, tiles, modes, LANES), f32),
            pltpu.VMEM((tiles, tokens, LANES), f32),
            pltpu.VMEM((ch_count, 2, half, channels), bf16),
            pltpu.VMEM((2, half, features), f32),
            pltpu.VMEM((SIDE, SIDE, part_rows, features), bf16),
            pltpu.VMEM((SIDE, SIDE, part_rows, features), bf16),
            pltpu.VMEM((ctx_count, ch_count, part_rows, features), bf16),
            dma((2 + ch_count,)),
            dma((6,)),
            dma((2, 2, SIDE)),
            dma((2, ctx_count // 2)),
            dma((2, ctx_count // 2)),
            dma((2, ctx_count)),
            dma((SIDE + 1, 2, 4)),
            dma((SIDE + 1, 2, 4)),
            dma((SIDE + 1, 2, 4)),
            dma((SIDE + 1, 2, 4)),
        ],
        compiler_params=pltpu.CompilerParams(
            collective_id=0, has_side_effects=True, vmem_limit_bytes=56 * 1024 * 1024
        ),
        cost_estimate=pl.CostEstimate(flops=flops, bytes_accessed=18 << 20, transcendentals=0),
    )(
        live_blocks,
        seq_lengths,
        norm_gain.reshape(ch_count, features),
        w_short,
        decay_rates,
        mode_weight,
        skip_gain.reshape(1, channels),
        x_owned,
        w_in,
        w_out,
    )


def solution(mesh):
    return jax.shard_map(
        body,
        mesh=mesh,
        in_specs=(
            P("ctx", "ch"),
            P(),
            P(),
            P(),
            P(None, None, "ch"),
            P(None, None, "ch"),
            P(None, "ch"),
            P(None, "ch"),
            P("ch"),
            P("ch", None),
        ),
        out_specs=P("ch", "ctx"),
        check_vma=False,
    )
```

time: 391 us -> 115 us (0.29)
  waiting for transfers between devices: 210 us -> 0 us
  Pallas kernels: 0 us -> 110 us
  local copies, waits for them, and re-layouts: 75.8 us -> 3.25 us
  matrix products: 47.4 us -> 0 us
  other arithmetic: 27.5 us -> 1.36 us
  between operations: 14.5 us -> 0.01 us
  blocking collectives: 9.95 us -> 0 us
  starting transfers between devices: 4.78 us -> 0 us
    all_gather x1 -> x0, waiting for transfers between devices: 116 us -> none  [project(): whole_rows = lax.all_gather(x_rows, 'ch', axis=1, tiled=True)]
    pallas_call x0 -> x1, Pallas kernels: none -> 110 us  [body(): pl.pallas_call(functools.partial(kernel, (ctx_count, tokens, block, width...]
    reduce_scatter x1 -> x0, waiting for transfers between devices: 82.6 us -> none  [body(): lax.psum_scatter(jnp.einsum('cd,ct->dt', w_out, tokens_out, preferred_ele...]
    dot_general x5 -> x0, matrix products: 47.4 us -> none  [the longest x1 27 us: project(): jnp.einsum('bdc,td->bct', w_in, normed, preferred_element_type=jnp.float32)]
    slice x27 -> x0, local copies, waits for them, and re-layouts: 42.3 us -> none  [the longest x23 38.2 us: local_pass(): lax.associative_scan(link_states, (block_steps, end_states), axis=2)]
    pad x6 -> x0, local copies, waits for them, and re-layouts: 14.7 us -> none  [local_pass(): lax.associative_scan(link_states, (block_steps, end_states), axis=2)]
    all_to_all x1 -> x0, waiting for transfers between devices: 10.7 us -> none  [to_channels(): lax.all_to_all(grouped, 'ctx', split_axis=1, concat_axis=3, tiled=True)]
    all_to_all x1 -> x0, blocking collectives: 9.95 us -> none  [to_tokens(): lax.all_to_all(gated_out.reshape(group_width, ctx_count, length // ctx_co...]
  transfers between devices with their start and end apart: 3 -> 0, of which waited for: 3 -> 0; matrix products, arithmetic and copies ran while one was open for 5% -> 0% of each run, Pallas kernels for 0% -> 0%
where the time goes in v1:
time: 115 us
  Pallas kernels  110 us (96%)
  local copies, waits for them, and re-layouts  3.25 us (3%)
  other arithmetic  1.36 us (1%)
    pallas_call x1, Pallas kernels, body(): pl.pallas_call(functools.partial(kernel, (ctx_count, tokens, block, width...  110 us

profile of v1, /device:TPU:0, one launch (start us, length us, event | category | flops | bytes accessed | tf_op | source)
XLA Modules:
  0.0 114.9 jit_solution(8355067320220204279)
XLA Ops:
  0.0 1.4 %sqrt_multiply_fusion.weight_ref = f32[16,256]{1,0:T(8,128)} fusion(f32[16,256]{1,0:T(8,128)} %param.17, f32[16,256]{1,0:T(8,128)} %rates_ref.1), kind=kLoop, calls=%fused_computation | loop fusion | flops 12288 | bytes 49152 | tf_op jit(solution)/shard_map/mul | solution.py:531
  1.4 1.4 %reshape.6.gain_ref = f32[16,512]{1,0:T(8,128)} reshape(f32[8192]{0:T(1024)} %param.13) | data formatting | bytes 65536 | tf_op jit(solution)/shard_map/reshape | solution.py:580
  2.7 110.3 %shard_map.100 = bf16[512,512]{1,0:T(8,128)(2,1)} custom-call(s32[8]{0:T(128)} %live_ref.1, s32[3]{0:T(128)} %lengths_ref.1, f32[16,512]{1,0:T(8,128)} %reshape.6.gain_ref, f32[3,3,256]{2,1,0:T(4,128)} %taps_ref.1, f32[16,256]{1,0:T(8,128)} %rates_ref.1, f32[16,256]{1,0:T(8,128)} %sqrt_multiply_fusion.weight_ref, f32[1,256]{1,0:T(1,128)} %bitcast.1, ...), custom_call_target="tpu_custom_call" | custom-call | flops 8589934592 | bytes 18874368 | tf_op jit(solution)/shard_map/pallas_call | solution.py:538
  113.0 1.9 %copy.12 = bf16[512,512]{1,0:T(8,128)(2,1)} copy(bf16[512,512]{1,0:T(8,128)(2,1)} %shard_map.100) | data formatting | bytes 1048576

commit v2 on v1

--- a/solution.py
+++ b/solution.py
@@ -96,12 +96,17 @@
         finish(0, h)
         send(4, h)
 
-    each(0, 2, open_rings)
-    each(0, 2, lambda h: use(h, place(h, 0, 0)))
-    each(0, 2, grow)
-    each(0, 4, lambda i: use(i // 2, piece(0, i // 2, 2 * (i % 2) - 1)))
-    each(0, 2, close_first)
-    each(0, 2, lambda h: use(h, piece(0, h, 2)))
+    def rest(opened, grown):
+        opened()
+        each(0, 2, lambda h: use(h, place(h, 0, 0)))
+        each(0, 2, grow)
+        grown()
+        each(0, 4, lambda i: use(i // 2, piece(0, i // 2, 2 * (i % 2) - 1)))
+        each(0, 2, close_first)
+        each(0, 2, lambda h: use(h, piece(0, h, 2)))
+        each(1, SIDE + 1, pass_on)
+        each(1, SIDE + 1, take_last)
+        each(0, 2, drain)
 
     def pass_on(ring):
         each(0, 2, lambda h: forward(ring, h))
@@ -110,9 +115,6 @@
     def take_last(ring):
         each(0, 2, lambda h: finish(ring, h))
         each(0, 2, lambda h: use(h, piece(ring, h, 2)))
-
-    each(1, SIDE + 1, pass_on)
-    each(1, SIDE + 1, take_last)
 
     def drain(index):
         h = index % 2
@@ -124,7 +126,7 @@
         for kind in range(4):
             copy(ring, h, kind, 0).wait_send()
 
-    each(0, 2, drain)
+    return open_rings, rest
 
 
 def kernel(
@@ -305,17 +307,19 @@
     own_x.start()
     own_x.wait()
 
-    to_next.wait_recv()
-    to_previous.wait_recv()
-    first_wanted = ctx * own_blocks
-    for i in range(own_blocks):
-        wanted = first_wanted + i
-        back = before - wanted
-        from_left = capacity + left_live - back - jnp.maximum(left_live - 2, 0)
-        from_right = capacity + 2 + wanted - before - here
-        source = jnp.where(wanted < before, from_left, jnp.where(wanted >= before + here, from_right, wanted - before))
-        nearby = list(range(max(i - 2, 0), min(i + 3, capacity))) + list(range(capacity, capacity + 4))
-        x_all[ch, (2 * i) // own_blocks, pl.ds((i * block) % half, block), :] = pick(source, nearby)
+    def fill(h):
+        for i in range(h * own_blocks // 2, (h + 1) * own_blocks // 2):
+            wanted = ctx * own_blocks + i
+            local = list(range(max(i - 2, 0), min(i + 3, capacity)))
+            if h == 0:
+                other = capacity + left_live - (before - wanted) - jnp.maximum(left_live - 2, 0)
+                source = jnp.where(wanted < before, other, wanted - before)
+                options = local + [capacity, capacity + 1]
+            else:
+                other = capacity + 2 + wanted - before - here
+                source = jnp.where(wanted >= before + here, other, wanted - before)
+                options = local + [capacity + 2, capacity + 3]
+            x_all[ch, h, pl.ds((i * block) % half, block), :] = pick(source, options)
 
     def project(h, g):
         wide = x_all[g, h].astype(jnp.float32)
@@ -325,31 +329,49 @@
             folded = folded + squared[:, lane * LANES : (lane + 1) * LANES]
         at = pl.ds(pl.multiple_of(h * half, half), half)
         squares[at, :] = squares[at, :] + folded
-        scaled = (wide * gain_ref[pl.ds(g, 1), :]).astype(jnp.bfloat16)
         deep = pl.ds(pl.multiple_of(g * features, features), features)
+        scaled = (wide * gain_ref[:, deep]).astype(jnp.bfloat16)
         for branch in range(BRANCHES):
             sums[branch, at, :] = sums[branch, at, :] + jnp.dot(
                 scaled, w_in[branch, deep, :], preferred_element_type=jnp.float32
             )
 
-    w_load.wait()
-    for step in range(1, SIDE):
-        along_x(step).wait_recv()
-    for step in range(1, SIDE):
-        along_y(step).start()
+    def second_leg():
+        for step in range(1, SIDE):
+            along_x(step).wait_recv()
+        for step in range(1, SIDE):
+            along_y(step).start()
+        own_y.start()
+        w_load.wait()
+
+    def third_leg():
+        for step in range(1, SIDE):
+            along_y(step).wait_recv()
+        own_y.wait()
+        for step in range(1, depth_count):
+            over_depth(step).start()
+        to_partner(0).start()
+
     own_y = pltpu.make_async_copy(w_half.at[:, row], w_mine.at[ctx, pl.ds(row * SIDE, SIDE)], local_sems.at[0])
-    own_y.start()
-    own_y.wait()
-    for step in range(1, SIDE):
-        along_y(step).wait_recv()
-    for step in range(1, depth_count):
-        over_depth(step).start()
-    to_partner(0).start()
-    plane_gather(x_all, x_send, x_recv, ctx, row, col, project)
-    for step in range(1, depth_count):
-        over_depth(depth_count - step).wait_recv()
-        to_partner(step).start()
-
+    open_x, rest_x = plane_gather(x_all, x_send, x_recv, ctx, row, col, project)
+    parity = lax.rem(ctx, 2)
+
+    def take(h):
+        @pl.when(h == 0)
+        def _():
+            to_next.wait_recv()
+            fill(0)
+
+        @pl.when(h == 1)
+        def _():
+            to_previous.wait_recv()
+            fill(1)
+
+        open_x(h)
+
+    take(1 - parity)
+    take(parity)
+    rest_x(second_leg, third_leg)
     def scale_rows(begin, count):
         total = jnp.sum(squares[pl.ds(begin, count), :], axis=1, keepdims=True)
         scale = lax.rsqrt(total / width + EPS)
@@ -416,7 +438,7 @@
         first = [proj[branch, tile, pl.ds(7, GROUPS, stride=run), :] for branch in range(BRANCHES)]
         second = [proj[branch, tile, pl.ds(6, GROUPS, stride=run), :] for branch in range(BRANCHES)]
         zero = jnp.zeros((GROUPS, LANES), jnp.float32)
-        done = lax.fori_loop(0, run, collect, ([zero] * modes, first, second, keep_at(-1)))
+        done = lax.fori_loop(0, run, collect, ([zero] * modes, first, second, keep_at(-1)), unroll=4)
         for m in range(modes):
             ends[tile, pl.ds(m * GROUPS, GROUPS), :] = done[0][m]
 
@@ -441,6 +463,9 @@
 
     for step in range(1, ctx_count):
         edge_to(step).start()
+    for step in range(1, depth_count):
+        over_depth(depth_count - step).wait_recv()
+        to_partner(step).start()
     for step in range(1, ctx_count):
         edge_to(step).wait_recv()
 
@@ -453,6 +478,13 @@
             starts[tile, pl.ds(i, modes, stride=GROUPS), :] = state
             if i < GROUPS - 1:
                 state = ends[tile, pl.ds(i, modes, stride=GROUPS), :] + (unbroken_run[i] * run_decay[tile]) * state
+
+    def multiply_out(h, g):
+        parts = LANES // part_rows
+        weights = w_mine[pl.ds(h * parts, parts), g].reshape(LANES, features)
+        out_sum[...] = out_sum[...] + jnp.dot(g_all[g, h], weights, preferred_element_type=jnp.float32)
+
+    open_g, rest_g = plane_gather(g_all, g_send, g_recv, ctx, row, col, multiply_out)
 
     for tile in range(tiles):
         lanes = pl.ds(tile * LANES, LANES)
@@ -474,22 +506,19 @@
             return states
 
         lax.fori_loop(
-            0, run, filtered, [starts[tile, pl.ds(m * GROUPS, GROUPS), :] for m in range(modes)]
-        )
-        for h in range(2):
-            g_all[ch, h, :, lanes] = mixed[tile, pl.ds(h * half, half), :].astype(jnp.bfloat16)
-
-    for step in range(1, depth_count):
-        to_partner(depth_count - step).wait_recv()
-    to_partner(0).wait_recv()
-
-    def multiply_out(h, g):
-        weights = w_mine[:, g].reshape(ctx_count * part_rows, features)
-        out_sum[h] = out_sum[h] + jnp.dot(g_all[g, h], weights, preferred_element_type=jnp.float32)
-
-    plane_gather(g_all, g_send, g_recv, ctx, row, col, multiply_out)
+            0, run, filtered, [starts[tile, pl.ds(m * GROUPS, GROUPS), :] for m in range(modes)], unroll=4
+        )
+        g_all[ch, tile] = mixed[tile].astype(jnp.bfloat16)
+        open_g(tile)
+
+    def last_leg():
+        for step in range(1, depth_count):
+            to_partner(depth_count - step).wait_recv()
+        to_partner(0).wait_recv()
+
+    rest_g(last_leg, lambda: None)
     for h in range(2):
-        out_ref[:, pl.ds(h * half, half)] = jnp.transpose(out_sum[h]).astype(jnp.bfloat16)
+        out_ref[:, pl.ds(h * half, half)] = jnp.transpose(out_sum[pl.ds(h * half, half), :]).astype(jnp.bfloat16)
 
     to_next.wait_send()
     to_previous.wait_send()
@@ -554,8 +583,8 @@
             pltpu.VMEM((tiles, modes * GROUPS, LANES), f32),
             pltpu.VMEM((ctx_count, tiles, modes, LANES), f32),
             pltpu.VMEM((tiles, tokens, LANES), f32),
-            pltpu.VMEM((ch_count, 2, half, channels), bf16),
-            pltpu.VMEM((2, half, features), f32),
+            pltpu.VMEM((ch_count, tiles, tokens, LANES), bf16),
+            pltpu.VMEM((tokens, features), f32),
             pltpu.VMEM((SIDE, SIDE, part_rows, features), bf16),
             pltpu.VMEM((SIDE, SIDE, part_rows, features), bf16),
             pltpu.VMEM((ctx_count, ch_count, part_rows, features), bf16),
@@ -577,7 +606,7 @@
     )(
         live_blocks,
         seq_lengths,
-        norm_gain.reshape(ch_count, features),
+        norm_gain.reshape(1, width),
         w_short,
         decay_rates,
         mode_weight,

time: 115 us -> 101 us (0.88)
  Pallas kernels: 110 us -> 97.3 us
  local copies, waits for them, and re-layouts: 3.25 us -> 1.87 us
    pallas_call x1, Pallas kernels: 110 us -> 97.3 us  [body(): pl.pallas_call(functools.partial(kernel, (ctx_count, tokens, block, width...]
    reshape x1 -> x0, local copies, waits for them, and re-layouts: 1.38 us -> none  [body(): norm_gain.reshape(ch_count, features)]
where the time goes in v2:
time: 101 us
  Pallas kernels  97.3 us (96%)
  local copies, waits for them, and re-layouts  1.87 us (2%)
  other arithmetic  1.36 us (1%)
    pallas_call x1, Pallas kernels, body(): pl.pallas_call(functools.partial(kernel, (ctx_count, tokens, block, width...  97.3 us

profile of v2, /device:TPU:0, one launch (start us, length us, event | category | flops | bytes accessed | tf_op | source)
XLA Modules:
  0.0 100.6 jit_solution(15317080355483611910)
XLA Ops:
  0.0 1.4 %sqrt_multiply_fusion.weight_ref = f32[16,256]{1,0:T(8,128)} fusion(f32[16,256]{1,0:T(8,128)} %param.17, f32[16,256]{1,0:T(8,128)} %rates_ref.1), kind=kLoop, calls=%fused_computation | loop fusion | flops 12288 | bytes 49152 | tf_op jit(solution)/shard_map/mul | solution.py:560
  1.4 97.3 %shard_map.100 = bf16[512,512]{1,0:T(8,128)(2,1)} custom-call(s32[8]{0:T(128)} %live_ref.1, s32[3]{0:T(128)} %lengths_ref.1, f32[1,8192]{1,0:T(1,128)} %bitcast.2, f32[3,3,256]{2,1,0:T(4,128)} %taps_ref.1, f32[16,256]{1,0:T(8,128)} %rates_ref.1, f32[16,256]{1,0:T(8,128)} %sqrt_multiply_fusion.weight_ref, f32[1,256]{1,0:T(1,128)} %bitcast.3, ...), custom_call_target="tpu_custom_call" | custom-call | flops 8589934592 | bytes 18874368 | tf_op jit(solution)/shard_map/pallas_call | solution.py:567
  98.7 1.9 %copy.12 = bf16[512,512]{1,0:T(8,128)(2,1)} copy(bf16[512,512]{1,0:T(8,128)(2,1)} %shard_map.100) | data formatting | bytes 1048576

commit v3 on v2

--- a/solution.py
+++ b/solution.py
@@ -133,11 +133,11 @@
     dims,
     live_ref,
     lengths_ref,
-    gain_ref,
-    taps_ref,
-    rates_ref,
-    weight_ref,
-    skip_ref,
+    gain_hbm,
+    taps_hbm,
+    rates_hbm,
+    residues_hbm,
+    skip_hbm,
     x_hbm,
     w_in_hbm,
     w_out_hbm,
@@ -160,6 +160,12 @@
     w_stage,
     w_half,
     w_mine,
+    gain_ref,
+    taps_ref,
+    rates_ref,
+    weight_ref,
+    skip_ref,
+    small_sems,
     local_sems,
     shift_sems,
     split_sems,
@@ -184,6 +190,18 @@
     part_rows = w_out_hbm.shape[0] // ctx_count
     half = tokens // 2
     modes = rates_ref.shape[0]
+    small = [
+        pltpu.make_async_copy(source, target, small_sems.at[i])
+        for i, (source, target) in enumerate(
+            (
+                (gain_hbm, gain_ref),
+                (taps_hbm, taps_ref),
+                (rates_hbm, rates_ref),
+                (residues_hbm, weight_ref),
+                (skip_hbm, skip_ref),
+            )
+        )
+    ]
     tiles = rates_ref.shape[1] // LANES
     run = tokens // GROUPS
 
@@ -205,6 +223,8 @@
             w_part(y * SIDE + x, w_stage.at[x, y], local_sems.at[2 + x * SIDE + y]).start()
     w_load = pltpu.make_async_copy(w_in_hbm, w_in, local_sems.at[1])
     w_load.start()
+    for copy in small:
+        copy.start()
 
     barrier = pltpu.get_barrier_semaphore()
     for step in range(1, SIDE):
@@ -258,28 +278,49 @@
     to_next.start()
     to_previous.start()
 
+    upper, lower = pl.ds(0, part_rows // 2), pl.ds(part_rows // 2, part_rows // 2)
     for x in range(SIDE):
         for y in range(SIDE):
             w_part(y * SIDE + x, w_stage.at[x, y], local_sems.at[2 + x * SIDE + y]).wait()
 
-    def along_x(step):
+    def first_x(step):
         x = lax.rem(col + step, SIDE)
         return remote(
-            w_stage.at[x],
-            w_half.at[col],
+            w_stage.at[x, :, upper],
+            w_half.at[0, col],
             split_sems.at[0, 0, step],
             split_sems.at[0, 1, step],
             (ctx, row * SIDE + x),
         )
 
-    def along_y(step):
+    def first_y(step):
         y = lax.rem(row + step, SIDE)
         return remote(
-            w_half.at[:, y],
-            w_mine.at[ctx, pl.ds(row * SIDE, SIDE)],
+            w_stage.at[:, y, lower],
+            w_half.at[1, row],
             split_sems.at[1, 0, step],
             split_sems.at[1, 1, step],
             (ctx, y * SIDE + col),
+        )
+
+    def then_y(step):
+        y = lax.rem(row + step, SIDE)
+        return remote(
+            w_half.at[0, :, y],
+            w_mine.at[ctx, row, :, upper],
+            split_sems.at[2, 0, step],
+            split_sems.at[2, 1, step],
+            (ctx, y * SIDE + col),
+        )
+
+    def then_x(step):
+        x = lax.rem(col + step, SIDE)
+        return remote(
+            w_half.at[1, :, x],
+            w_mine.at[ctx, :, col, lower],
+            split_sems.at[3, 0, step],
+            split_sems.at[3, 1, step],
+            (ctx, row * SIDE + x),
         )
 
     def over_depth(step):
@@ -301,11 +342,17 @@
             (partner, ch),
         )
 
-    for step in range(1, SIDE):
-        along_x(step).start()
-    own_x = pltpu.make_async_copy(w_stage.at[col], w_half.at[col], local_sems.at[0])
-    own_x.start()
-    own_x.wait()
+    for step in (1, 3, 2):
+        first_x(step).start()
+        first_y(step).start()
+    kept = (
+        pltpu.make_async_copy(w_stage.at[col, :, upper], w_half.at[0, col], local_sems.at[0]),
+        pltpu.make_async_copy(w_stage.at[:, row, lower], w_half.at[1, row], local_sems.at[2]),
+        pltpu.make_async_copy(w_half.at[0, :, row], w_mine.at[ctx, row, :, upper], local_sems.at[3]),
+        pltpu.make_async_copy(w_half.at[1, :, col], w_mine.at[ctx, :, col, lower], local_sems.at[4]),
+    )
+    kept[0].start()
+    kept[1].start()
 
     def fill(h):
         for i in range(h * own_blocks // 2, (h + 1) * own_blocks // 2):
@@ -337,22 +384,36 @@
             )
 
     def second_leg():
+        kept[0].wait()
+        kept[1].wait()
         for step in range(1, SIDE):
-            along_x(step).wait_recv()
-        for step in range(1, SIDE):
-            along_y(step).start()
-        own_y.start()
+            first_x(step).wait_recv()
+            first_y(step).wait_recv()
+        for step in (1, 3, 2):
+            then_y(step).start()
+            then_x(step).start()
+        kept[2].start()
+        kept[3].start()
         w_load.wait()
+        for copy in small:
+            copy.wait()
+        doubled = 2.0 * rates_ref[...]
+        series = jnp.ones_like(doubled)
+        for order in range(8, 1, -1):
+            series = 1.0 - doubled * (1.0 / order) * series
+        risen = jnp.where(doubled < 0.1, doubled * series, 1.0 - jnp.exp(-doubled))
+        weight_ref[...] = weight_ref[...] * jnp.sqrt(risen)
 
     def third_leg():
         for step in range(1, SIDE):
-            along_y(step).wait_recv()
-        own_y.wait()
+            then_y(step).wait_recv()
+            then_x(step).wait_recv()
+        kept[2].wait()
+        kept[3].wait()
         for step in range(1, depth_count):
             over_depth(step).start()
         to_partner(0).start()
 
-    own_y = pltpu.make_async_copy(w_half.at[:, row], w_mine.at[ctx, pl.ds(row * SIDE, SIDE)], local_sems.at[0])
     open_x, rest_x = plane_gather(x_all, x_send, x_recv, ctx, row, col, project)
     parity = lax.rem(ctx, 2)
 
@@ -410,7 +471,22 @@
     def spread_row(values):
         return jnp.broadcast_to(values, (GROUPS, LANES))
 
-    for tile in range(tiles):
+    run_decay = [jnp.exp(-run * rates_ref[:, pl.ds(tile * LANES, LANES)]) for tile in range(tiles)]
+    all_decay = [jnp.exp(-tokens * rates_ref[:, pl.ds(tile * LANES, LANES)]) for tile in range(tiles)]
+    unbroken_run = [unbroken(base + run * i, run) for i in range(GROUPS)]
+
+    unbroken_device = [unbroken(jnp.int32(device * tokens), tokens) for device in range(ctx_count)]
+
+    def edge_to(step, tile):
+        return remote(
+            edge.at[ctx, tile],
+            edge.at[ctx, tile],
+            edge_sems.at[0, tile, step],
+            edge_sems.at[1, tile, step],
+            (lax.rem(ctx + step, ctx_count), ch),
+        )
+
+    def first_pass(tile):
         lanes = pl.ds(tile * LANES, LANES)
         decays = [spread_row(jnp.exp(-rates_ref[pl.ds(m, 1), lanes])) for m in range(modes)]
         taps = [
@@ -418,7 +494,7 @@
             for tap in range(TAPS)
         ]
 
-        def collect(t, carry, tile=tile, decays=decays, taps=taps):
+        def collect(t, carry, decays=decays, taps=taps):
             states, one_back, two_back, keep_before = carry
             keep = keep_at(t)
             far = keep * keep_before
@@ -441,58 +517,37 @@
         done = lax.fori_loop(0, run, collect, ([zero] * modes, first, second, keep_at(-1)), unroll=4)
         for m in range(modes):
             ends[tile, pl.ds(m * GROUPS, GROUPS), :] = done[0][m]
-
-    run_decay = [jnp.exp(-run * rates_ref[:, pl.ds(tile * LANES, LANES)]) for tile in range(tiles)]
-    all_decay = [jnp.exp(-tokens * rates_ref[:, pl.ds(tile * LANES, LANES)]) for tile in range(tiles)]
-    unbroken_run = [unbroken(base + run * i, run) for i in range(GROUPS)]
-
-    for tile in range(tiles):
         state = jnp.zeros((modes, LANES), jnp.float32)
         for i in range(GROUPS):
             state = ends[tile, pl.ds(i, modes, stride=GROUPS), :] + (unbroken_run[i] * run_decay[tile]) * state
         edge[ctx, tile] = state
-
-    def edge_to(step):
-        return remote(
-            edge.at[ctx],
-            edge.at[ctx],
-            edge_sems.at[0, step],
-            edge_sems.at[1, step],
-            (lax.rem(ctx + step, ctx_count), ch),
-        )
-
-    for step in range(1, ctx_count):
-        edge_to(step).start()
-    for step in range(1, depth_count):
-        over_depth(depth_count - step).wait_recv()
-        to_partner(step).start()
-    for step in range(1, ctx_count):
-        edge_to(step).wait_recv()
-
-    for tile in range(tiles):
+        for step in range(1, ctx_count):
+            edge_to(step, tile).start()
+
+    def multiply_out(h, g):
+        parts = LANES // part_rows
+        weights = w_mine[pl.ds(h * parts, parts), g // SIDE, lax.rem(g, SIDE)].reshape(LANES, features)
+        out_sum[...] = out_sum[...] + jnp.dot(g_all[g, h], weights, preferred_element_type=jnp.float32)
+
+    open_g, rest_g = plane_gather(g_all, g_send, g_recv, ctx, row, col, multiply_out)
+
+    def second_pass(tile):
+        for step in range(1, ctx_count):
+            edge_to(step, tile).wait_recv()
         state = jnp.zeros((modes, LANES), jnp.float32)
         for device in range(ctx_count):
-            moved = edge[device, tile] + (unbroken(jnp.int32(device * tokens), tokens) * all_decay[tile]) * state
+            moved = edge[device, tile] + (unbroken_device[device] * all_decay[tile]) * state
             state = jnp.where(device < ctx, moved, state)
         for i in range(GROUPS):
             starts[tile, pl.ds(i, modes, stride=GROUPS), :] = state
             if i < GROUPS - 1:
                 state = ends[tile, pl.ds(i, modes, stride=GROUPS), :] + (unbroken_run[i] * run_decay[tile]) * state
-
-    def multiply_out(h, g):
-        parts = LANES // part_rows
-        weights = w_mine[pl.ds(h * parts, parts), g].reshape(LANES, features)
-        out_sum[...] = out_sum[...] + jnp.dot(g_all[g, h], weights, preferred_element_type=jnp.float32)
-
-    open_g, rest_g = plane_gather(g_all, g_send, g_recv, ctx, row, col, multiply_out)
-
-    for tile in range(tiles):
         lanes = pl.ds(tile * LANES, LANES)
         decays = [spread_row(jnp.exp(-rates_ref[pl.ds(m, 1), lanes])) for m in range(modes)]
         weights = [spread_row(weight_ref[pl.ds(m, 1), lanes]) for m in range(modes)]
         direct = spread_row(skip_ref[:, lanes])
 
-        def filtered(t, states, tile=tile, decays=decays, weights=weights, direct=direct):
+        def filtered(t, states, decays=decays, weights=weights, direct=direct):
             keep = keep_at(t)
             entered = gated[tile, t]
             states = [decays[m] * (states[m] * keep) + entered for m in range(modes)]
@@ -511,6 +566,14 @@
         g_all[ch, tile] = mixed[tile].astype(jnp.bfloat16)
         open_g(tile)
 
+    for tile in range(tiles):
+        first_pass(tile)
+    for step in range(1, depth_count):
+        over_depth(depth_count - step).wait_recv()
+        to_partner(step).start()
+    for tile in range(tiles):
+        second_pass(tile)
+
     def last_leg():
         for step in range(1, depth_count):
             to_partner(depth_count - step).wait_recv()
@@ -524,14 +587,17 @@
     to_previous.wait_send()
     halo.wait_send()
     for step in range(1, SIDE):
-        along_x(step).wait_send()
-        along_y(step).wait_send()
+        first_x(step).wait_send()
+        first_y(step).wait_send()
+        then_y(step).wait_send()
+        then_x(step).wait_send()
     for step in range(1, depth_count):
         over_depth(step).wait_send()
     for step in range(depth_count):
         to_partner(step).wait_send()
     for step in range(1, ctx_count):
-        edge_to(step).wait_send()
+        for tile in range(tiles):
+            edge_to(step, tile).wait_send()
 
 
 def body(
@@ -557,7 +623,6 @@
     modes, channels = decay_rates.shape
     tiles = channels // LANES
     part_rows = channels // ctx_count
-    mode_weight = residues * jnp.sqrt(-jnp.expm1(-2.0 * decay_rates))
     bf16, f32 = jnp.bfloat16, jnp.float32
     smem = pl.BlockSpec(memory_space=pltpu.SMEM)
     vmem = pl.BlockSpec(memory_space=pltpu.VMEM)
@@ -567,7 +632,7 @@
     return pl.pallas_call(
         functools.partial(kernel, (ctx_count, tokens, block, width)),
         out_shape=jax.ShapeDtypeStruct((features, tokens), bf16),
-        in_specs=[smem, smem, vmem, vmem, vmem, vmem, vmem, anywhere, anywhere, anywhere],
+        in_specs=[smem, smem] + [anywhere] * 8,
         out_specs=vmem,
         scratch_shapes=[
             pltpu.VMEM((x_owned.shape[0] + 4 * block, features), bf16),
@@ -586,14 +651,20 @@
             pltpu.VMEM((ch_count, tiles, tokens, LANES), bf16),
             pltpu.VMEM((tokens, features), f32),
             pltpu.VMEM((SIDE, SIDE, part_rows, features), bf16),
-            pltpu.VMEM((SIDE, SIDE, part_rows, features), bf16),
-            pltpu.VMEM((ctx_count, ch_count, part_rows, features), bf16),
+            pltpu.VMEM((2, SIDE, SIDE, part_rows // 2, features), bf16),
+            pltpu.VMEM((ctx_count, SIDE, SIDE, part_rows, features), bf16),
+            pltpu.VMEM((1, width), f32),
+            pltpu.VMEM((TAPS, BRANCHES, channels), f32),
+            pltpu.VMEM((modes, channels), f32),
+            pltpu.VMEM((modes, channels), f32),
+            pltpu.VMEM((1, channels), f32),
+            dma((5,)),
             dma((2 + ch_count,)),
             dma((6,)),
-            dma((2, 2, SIDE)),
+            dma((4, 2, SIDE)),
             dma((2, ctx_count // 2)),
             dma((2, ctx_count // 2)),
-            dma((2, ctx_count)),
+            dma((2, tiles, ctx_count)),
             dma((SIDE + 1, 2, 4)),
             dma((SIDE + 1, 2, 4)),
             dma((SIDE + 1, 2, 4)),
@@ -609,7 +680,7 @@
         norm_gain.reshape(1, width),
         w_short,
         decay_rates,
-        mode_weight,
+        residues,
         skip_gain.reshape(1, channels),
         x_owned,
         w_in,

time: 101 us -> 98.1 us (0.971)
  other arithmetic: 1.36 us -> 0 us
  Pallas kernels: 97.3 us -> 96 us
    pallas_call x1, Pallas kernels: 97.3 us -> 96 us  [body(): pl.pallas_call(functools.partial(kernel, (ctx_count, tokens, block, width...]
    mul x1 -> x0, other arithmetic: 1.36 us -> none  [body(): mode_weight = residues * jnp.sqrt(-jnp.expm1(-2.0 * decay_rates))]
where the time goes in v3:
time: 98.1 us; the launch traced here: 97.8 us
  Pallas kernels  96 us (98%)
  local copies, waits for them, and re-layouts  1.87 us (2%)
    pallas_call x1, Pallas kernels, body(): pl.pallas_call(functools.partial(kernel, (ctx_count, tokens, block, width...  96 us

profile of v3, /device:TPU:0, one launch (start us, length us, event | category | flops | bytes accessed | tf_op | source)
XLA Modules:
  0.0 97.8 jit_solution(14564122779474998689)
XLA Ops:
  0.0 96.0 %shard_map.100 = bf16[512,512]{1,0:T(8,128)(2,1)} custom-call(s32[8]{0:T(128)} %live_ref.1, s32[3]{0:T(128)} %lengths_ref.1, f32[1,8192]{1,0:T(1,128)} %bitcast.2, f32[3,3,256]{2,1,0:T(4,128)} %taps_hbm.1, f32[16,256]{1,0:T(8,128)} %rates_hbm.1, f32[16,256]{1,0:T(8,128)} %residues_hbm.1, f32[1,256]{1,0:T(1,128)} %bitcast.3, bf16[1024,512]{1,0:T(8,128)(2,1)} %x_hbm.1, ...), custom_call_target="tpu_custom_call" | custom-call | flops 8589934592 | bytes 18874368 | tf_op jit(solution)/shard_map/pallas_call | solution.py:632
  96.0 1.9 %copy.12 = bf16[512,512]{1,0:T(8,128)(2,1)} copy(bf16[512,512]{1,0:T(8,128)(2,1)} %shard_map.100) | data formatting | bytes 1048576

commit v4 on v3

--- a/solution.py
+++ b/solution.py
@@ -96,25 +96,52 @@
         finish(0, h)
         send(4, h)
 
-    def rest(opened, grown):
-        opened()
-        each(0, 2, lambda h: use(h, place(h, 0, 0)))
-        each(0, 2, grow)
-        grown()
-        each(0, 4, lambda i: use(i // 2, piece(0, i // 2, 2 * (i % 2) - 1)))
-        each(0, 2, close_first)
-        each(0, 2, lambda h: use(h, piece(0, h, 2)))
-        each(1, SIDE + 1, pass_on)
-        each(1, SIDE + 1, take_last)
-        each(0, 2, drain)
+    def forward_both(ring):
+        each(0, 2, lambda h: forward(ring, h))
+
+    def use_sides(ring):
+        each(0, 4, lambda i: use(i // 2, piece(ring, i // 2, 2 * (i % 2) - 1)))
 
     def pass_on(ring):
-        each(0, 2, lambda h: forward(ring, h))
-        each(0, 4, lambda i: use(i // 2, piece(ring, i // 2, 2 * (i % 2) - 1)))
+        forward_both(ring)
+        use_sides(ring)
 
     def take_last(ring):
         each(0, 2, lambda h: finish(ring, h))
         each(0, 2, lambda h: use(h, piece(ring, h, 2)))
+
+    def use_own():
+        each(0, 2, lambda h: use(h, place(h, 0, 0)))
+
+    def use_opposite():
+        each(0, 2, lambda h: use(h, piece(0, h, 2)))
+
+    def use_as_it_comes(opened, passed):
+        opened()
+        use_own()
+        each(0, 2, grow)
+        use_sides(0)
+        each(0, 2, close_first)
+        use_opposite()
+        each(1, SIDE + 1, pass_on)
+        passed()
+        each(1, SIDE + 1, take_last)
+        each(0, 2, drain)
+
+    def use_when_ready(grown, nearly, ready):
+        each(0, 2, grow)
+        grown()
+        each(0, 2, close_first)
+        each(1, SIDE, forward_both)
+        nearly()
+        each(SIDE, SIDE + 1, forward_both)
+        ready()
+        use_own()
+        use_sides(0)
+        use_opposite()
+        each(1, SIDE + 1, use_sides)
+        each(1, SIDE + 1, take_last)
+        each(0, 2, drain)
 
     def drain(index):
         h = index % 2
@@ -126,7 +153,7 @@
         for kind in range(4):
             copy(ring, h, kind, 0).wait_send()
 
-    return open_rings, rest
+    return open_rings, use_as_it_comes, use_when_ready
 
 
 def kernel(
@@ -323,14 +350,12 @@
             (ctx, row * SIDE + x),
         )
 
-    def over_depth(step):
-        return remote(
-            w_mine.at[ctx],
-            w_mine.at[ctx],
-            deep_sems.at[0, step],
-            deep_sems.at[1, step],
-            (lax.rem(ctx + 2 * step, ctx_count), ch),
-        )
+    def over_depth(kind):
+        shift = 2 * (1 - 2 * (kind % 2))
+        target = lax.rem(ctx + ctx_count + shift, ctx_count)
+        held = ctx if kind < 2 else lax.rem(ctx + ctx_count - shift, ctx_count)
+        part = w_mine.at[held, pl.ds((0, 0, 0, SIDE // 2)[kind], (SIDE, SIDE, SIDE // 2, SIDE // 2)[kind])]
+        return remote(part, part, deep_sems.at[0, kind], deep_sems.at[1, kind], (target, ch))
 
     def to_partner(step):
         held = lax.rem(ctx + 2 * step, ctx_count)
@@ -342,18 +367,12 @@
             (partner, ch),
         )
 
-    for step in (1, 3, 2):
-        first_x(step).start()
-        first_y(step).start()
     kept = (
         pltpu.make_async_copy(w_stage.at[col, :, upper], w_half.at[0, col], local_sems.at[0]),
         pltpu.make_async_copy(w_stage.at[:, row, lower], w_half.at[1, row], local_sems.at[2]),
         pltpu.make_async_copy(w_half.at[0, :, row], w_mine.at[ctx, row, :, upper], local_sems.at[3]),
         pltpu.make_async_copy(w_half.at[1, :, col], w_mine.at[ctx, :, col, lower], local_sems.at[4]),
     )
-    kept[0].start()
-    kept[1].start()
-
     def fill(h):
         for i in range(h * own_blocks // 2, (h + 1) * own_blocks // 2):
             wanted = ctx * own_blocks + i
@@ -383,6 +402,24 @@
                 scaled, w_in[branch, deep, :], preferred_element_type=jnp.float32
             )
 
+    def ready_weights():
+        w_load.wait()
+        for copy in small:
+            copy.wait()
+        doubled = 2.0 * rates_ref[...]
+        series = jnp.ones_like(doubled)
+        for order in range(8, 1, -1):
+            series = 1.0 - doubled * (1.0 / order) * series
+        risen = jnp.where(doubled < 0.1, doubled * series, 1.0 - jnp.exp(-doubled))
+        weight_ref[...] = weight_ref[...] * jnp.sqrt(risen)
+
+    def first_leg():
+        for step in (1, 3, 2):
+            first_x(step).start()
+            first_y(step).start()
+        kept[0].start()
+        kept[1].start()
+
     def second_leg():
         kept[0].wait()
         kept[1].wait()
@@ -394,15 +431,6 @@
             then_x(step).start()
         kept[2].start()
         kept[3].start()
-        w_load.wait()
-        for copy in small:
-            copy.wait()
-        doubled = 2.0 * rates_ref[...]
-        series = jnp.ones_like(doubled)
-        for order in range(8, 1, -1):
-            series = 1.0 - doubled * (1.0 / order) * series
-        risen = jnp.where(doubled < 0.1, doubled * series, 1.0 - jnp.exp(-doubled))
-        weight_ref[...] = weight_ref[...] * jnp.sqrt(risen)
 
     def third_leg():
         for step in range(1, SIDE):
@@ -410,11 +438,24 @@
             then_x(step).wait_recv()
         kept[2].wait()
         kept[3].wait()
-        for step in range(1, depth_count):
-            over_depth(step).start()
+        over_depth(0).start()
+        over_depth(1).start()
         to_partner(0).start()
 
-    open_x, rest_x = plane_gather(x_all, x_send, x_recv, ctx, row, col, project)
+    def fourth_leg():
+        over_depth(0).wait_recv()
+        over_depth(2).start()
+        over_depth(1).wait_recv()
+        over_depth(3).start()
+        to_partner(1).start()
+        to_partner(depth_count - 1).start()
+
+    def fifth_leg():
+        over_depth(2).wait_recv()
+        over_depth(3).wait_recv()
+        to_partner(2).start()
+
+    open_x, rest_x, _ = plane_gather(x_all, x_send, x_recv, ctx, row, col, project)
     parity = lax.rem(ctx, 2)
 
     def take(h):
@@ -432,7 +473,7 @@
 
     take(1 - parity)
     take(parity)
-    rest_x(second_leg, third_leg)
+    rest_x(ready_weights, first_leg)
     def scale_rows(begin, count):
         total = jnp.sum(squares[pl.ds(begin, count), :], axis=1, keepdims=True)
         scale = lax.rsqrt(total / width + EPS)
@@ -452,6 +493,7 @@
     )
     halo.start()
     each(0, GROUPS - 1, lambda i: scale_rows(pl.multiple_of(i * run, run), run))
+    second_leg()
     halo.wait_recv()
 
     cut_one = lengths_ref[0]
@@ -529,7 +571,7 @@
         weights = w_mine[pl.ds(h * parts, parts), g // SIDE, lax.rem(g, SIDE)].reshape(LANES, features)
         out_sum[...] = out_sum[...] + jnp.dot(g_all[g, h], weights, preferred_element_type=jnp.float32)
 
-    open_g, rest_g = plane_gather(g_all, g_send, g_recv, ctx, row, col, multiply_out)
+    open_g, _, rest_g = plane_gather(g_all, g_send, g_recv, ctx, row, col, multiply_out)
 
     def second_pass(tile):
         for step in range(1, ctx_count):
@@ -568,9 +610,7 @@
 
     for tile in range(tiles):
         first_pass(tile)
-    for step in range(1, depth_count):
-        over_depth(depth_count - step).wait_recv()
-        to_partner(step).start()
+    third_leg()
     for tile in range(tiles):
         second_pass(tile)
 
@@ -579,7 +619,7 @@
             to_partner(depth_count - step).wait_recv()
         to_partner(0).wait_recv()
 
-    rest_g(last_leg, lambda: None)
+    rest_g(fourth_leg, fifth_leg, last_leg)
     for h in range(2):
         out_ref[:, pl.ds(h * half, half)] = jnp.transpose(out_sum[pl.ds(h * half, half), :]).astype(jnp.bfloat16)
 
@@ -591,8 +631,8 @@
         first_y(step).wait_send()
         then_y(step).wait_send()
         then_x(step).wait_send()
-    for step in range(1, depth_count):
-        over_depth(step).wait_send()
+    for kind in range(4):
+        over_depth(kind).wait_send()
     for step in range(depth_count):
         to_partner(step).wait_send()
     for step in range(1, ctx_count):
@@ -662,7 +702,7 @@
             dma((2 + ch_count,)),
             dma((6,)),
             dma((4, 2, SIDE)),
-            dma((2, ctx_count // 2)),
+            dma((2, 4)),
             dma((2, ctx_count // 2)),
             dma((2, tiles, ctx_count)),
             dma((SIDE + 1, 2, 4)),

time: 98.1 us -> 101 us (1.030)
  Pallas kernels: 96 us -> 99.3 us
    pallas_call x1, Pallas kernels: 96 us -> 99.3 us  [body(): pl.pallas_call(functools.partial(kernel, (ctx_count, tokens, block, width...]
where the time goes in v4:
time: 101 us
  Pallas kernels  99.3 us (98%)
  local copies, waits for them, and re-layouts  1.87 us (2%)
    pallas_call x1, Pallas kernels, body(): pl.pallas_call(functools.partial(kernel, (ctx_count, tokens, block, width...  99.3 us

profile of v4, /device:TPU:0, one launch (start us, length us, event | category | flops | bytes accessed | tf_op | source)
XLA Modules:
  0.0 101.2 jit_solution(11088744516565138274)
XLA Ops:
  0.0 99.3 %shard_map.100 = bf16[512,512]{1,0:T(8,128)(2,1)} custom-call(s32[8]{0:T(128)} %live_ref.1, s32[3]{0:T(128)} %lengths_ref.1, f32[1,8192]{1,0:T(1,128)} %bitcast.2, f32[3,3,256]{2,1,0:T(4,128)} %taps_hbm.1, f32[16,256]{1,0:T(8,128)} %rates_hbm.1, f32[16,256]{1,0:T(8,128)} %residues_hbm.1, f32[1,256]{1,0:T(1,128)} %bitcast.3, bf16[1024,512]{1,0:T(8,128)(2,1)} %x_hbm.1, ...), custom_call_target="tpu_custom_call" | custom-call | flops 8589934592 | bytes 18874368 | tf_op jit(solution)/shard_map/pallas_call | solution.py:672
  99.3 1.9 %copy.12 = bf16[512,512]{1,0:T(8,128)(2,1)} copy(bf16[512,512]{1,0:T(8,128)(2,1)} %shard_map.100) | data formatting | bytes 1048576

commit v5 on v3

--- a/solution.py
+++ b/solution.py
@@ -452,7 +452,6 @@
     )
     halo.start()
     each(0, GROUPS - 1, lambda i: scale_rows(pl.multiple_of(i * run, run), run))
-    halo.wait_recv()
 
     cut_one = lengths_ref[0]
     cut_two = cut_one + lengths_ref[1]
@@ -495,7 +494,7 @@
         ]
 
         def collect(t, carry, decays=decays, taps=taps):
-            states, one_back, two_back, keep_before = carry
+            states, one_back, two_back, keep_before, alive = carry
             keep = keep_at(t)
             far = keep * keep_before
             now = [proj[branch, tile, pl.ds(8 + t, GROUPS, stride=run), :] for branch in range(BRANCHES)]
@@ -509,14 +508,24 @@
             query[tile, t] = parts[0]
             gated[tile, t] = entered
             states = [decays[m] * (states[m] * keep) + entered for m in range(modes)]
-            return (states, now, one_back, keep)
-
-        first = [proj[branch, tile, pl.ds(7, GROUPS, stride=run), :] for branch in range(BRANCHES)]
-        second = [proj[branch, tile, pl.ds(6, GROUPS, stride=run), :] for branch in range(BRANCHES)]
+            return (states, now, one_back, keep, alive * keep)
+
+        def rows_at(t):
+            return [proj[branch, tile, pl.ds(8 + t, GROUPS, stride=run), :] for branch in range(BRANCHES)]
+
         zero = jnp.zeros((GROUPS, LANES), jnp.float32)
-        done = lax.fori_loop(0, run, collect, ([zero] * modes, first, second, keep_at(-1)), unroll=4)
+        one = jnp.ones((GROUPS, LANES), jnp.float32)
+        later = lax.fori_loop(
+            2, run, collect, ([zero] * modes, rows_at(1), rows_at(0), keep_at(1), one), unroll=2
+        )
+        if tile == 0:
+            halo.wait_recv()
+        begun = ([zero] * modes, rows_at(-1), rows_at(-2), keep_at(-1), one)
+        for t in range(2):
+            begun = collect(t, begun)
         for m in range(modes):
-            ends[tile, pl.ds(m * GROUPS, GROUPS), :] = done[0][m]
+            fall = spread_row(jnp.exp(-(run - 2.0) * rates_ref[pl.ds(m, 1), lanes]))
+            ends[tile, pl.ds(m * GROUPS, GROUPS), :] = later[0][m] + fall * (later[4] * begun[0][m])
         state = jnp.zeros((modes, LANES), jnp.float32)
         for i in range(GROUPS):
             state = ends[tile, pl.ds(i, modes, stride=GROUPS), :] + (unbroken_run[i] * run_decay[tile]) * state

time: 98.1 us -> 97.8 us (level)
  no operation moved by 1% of the time
where the time goes in v5:
time: 97.8 us; the launch traced here: 97.6 us
  Pallas kernels  95.7 us (98%)
  local copies, waits for them, and re-layouts  1.87 us (2%)
    pallas_call x1, Pallas kernels, body(): pl.pallas_call(functools.partial(kernel, (ctx_count, tokens, block, width...  95.7 us

profile of v5, /device:TPU:0, one launch (start us, length us, event | category | flops | bytes accessed | tf_op | source)
XLA Modules:
  0.0 97.6 jit_solution(2456032106350764854)
XLA Ops:
  0.0 95.7 %shard_map.100 = bf16[512,512]{1,0:T(8,128)(2,1)} custom-call(s32[8]{0:T(128)} %live_ref.1, s32[3]{0:T(128)} %lengths_ref.1, f32[1,8192]{1,0:T(1,128)} %bitcast.2, f32[3,3,256]{2,1,0:T(4,128)} %taps_hbm.1, f32[16,256]{1,0:T(8,128)} %rates_hbm.1, f32[16,256]{1,0:T(8,128)} %residues_hbm.1, f32[1,256]{1,0:T(1,128)} %bitcast.3, bf16[1024,512]{1,0:T(8,128)(2,1)} %x_hbm.1, ...), custom_call_target="tpu_custom_call" | custom-call | flops 8589934592 | bytes 18874368 | tf_op jit(solution)/shard_map/pallas_call | solution.py:641
  95.7 1.9 %copy.12 = bf16[512,512]{1,0:T(8,128)(2,1)} copy(bf16[512,512]{1,0:T(8,128)(2,1)} %shard_map.100) | data formatting | bytes 1048576

commit v6 on v5

--- a/solution.py
+++ b/solution.py
@@ -96,15 +96,17 @@
         finish(0, h)
         send(4, h)
 
-    def rest(opened, grown):
+    def rest(opened, begun, passed):
         opened()
         each(0, 2, lambda h: use(h, place(h, 0, 0)))
         each(0, 2, grow)
-        grown()
         each(0, 4, lambda i: use(i // 2, piece(0, i // 2, 2 * (i % 2) - 1)))
         each(0, 2, close_first)
         each(0, 2, lambda h: use(h, piece(0, h, 2)))
-        each(1, SIDE + 1, pass_on)
+        each(1, 2, pass_on)
+        begun()
+        each(2, SIDE + 1, pass_on)
+        passed()
         each(1, SIDE + 1, take_last)
         each(0, 2, drain)
 
@@ -323,14 +325,12 @@
             (ctx, row * SIDE + x),
         )
 
-    def over_depth(step):
-        return remote(
-            w_mine.at[ctx],
-            w_mine.at[ctx],
-            deep_sems.at[0, step],
-            deep_sems.at[1, step],
-            (lax.rem(ctx + 2 * step, ctx_count), ch),
-        )
+    def over_depth(kind):
+        shift = 2 * (1 - 2 * (kind % 2))
+        target = lax.rem(ctx + ctx_count + shift, ctx_count)
+        held = ctx if kind < 2 else lax.rem(ctx + ctx_count - shift, ctx_count)
+        part = w_mine.at[held, pl.ds((0, 0, 0, SIDE // 2)[kind], (SIDE, SIDE, SIDE // 2, SIDE // 2)[kind])]
+        return remote(part, part, deep_sems.at[0, kind], deep_sems.at[1, kind], (target, ch))
 
     def to_partner(step):
         held = lax.rem(ctx + 2 * step, ctx_count)
@@ -410,9 +410,17 @@
             then_x(step).wait_recv()
         kept[2].wait()
         kept[3].wait()
-        for step in range(1, depth_count):
-            over_depth(step).start()
+        over_depth(0).start()
+        over_depth(1).start()
         to_partner(0).start()
+
+    def fourth_leg():
+        over_depth(0).wait_recv()
+        over_depth(2).start()
+        over_depth(1).wait_recv()
+        over_depth(3).start()
+        to_partner(1).start()
+        to_partner(depth_count - 1).start()
 
     open_x, rest_x = plane_gather(x_all, x_send, x_recv, ctx, row, col, project)
     parity = lax.rem(ctx, 2)
@@ -432,7 +440,7 @@
 
     take(1 - parity)
     take(parity)
-    rest_x(second_leg, third_leg)
+    rest_x(second_leg, third_leg, fourth_leg)
     def scale_rows(begin, count):
         total = jnp.sum(squares[pl.ds(begin, count), :], axis=1, keepdims=True)
         scale = lax.rsqrt(total / width + EPS)
@@ -577,9 +585,9 @@
 
     for tile in range(tiles):
         first_pass(tile)
-    for step in range(1, depth_count):
-        over_depth(depth_count - step).wait_recv()
-        to_partner(step).start()
+    over_depth(2).wait_recv()
+    over_depth(3).wait_recv()
+    to_partner(2).start()
     for tile in range(tiles):
         second_pass(tile)
 
@@ -588,7 +596,7 @@
             to_partner(depth_count - step).wait_recv()
         to_partner(0).wait_recv()
 
-    rest_g(last_leg, lambda: None)
+    rest_g(last_leg, lambda: None, lambda: None)
     for h in range(2):
         out_ref[:, pl.ds(h * half, half)] = jnp.transpose(out_sum[pl.ds(h * half, half), :]).astype(jnp.bfloat16)
 
@@ -600,8 +608,8 @@
         first_y(step).wait_send()
         then_y(step).wait_send()
         then_x(step).wait_send()
-    for step in range(1, depth_count):
-        over_depth(step).wait_send()
+    for kind in range(4):
+        over_depth(kind).wait_send()
     for step in range(depth_count):
         to_partner(step).wait_send()
     for step in range(1, ctx_count):
@@ -671,7 +679,7 @@
             dma((2 + ch_count,)),
             dma((6,)),
             dma((4, 2, SIDE)),
-            dma((2, ctx_count // 2)),
+            dma((2, 4)),
             dma((2, ctx_count // 2)),
             dma((2, tiles, ctx_count)),
             dma((SIDE + 1, 2, 4)),

time: 97.8 us -> 97.9 us (level)
  no operation moved by 1% of the time
where the time goes in v6:
time: 97.9 us; the launch traced here: 97.7 us
  Pallas kernels  95.9 us (98%)
  local copies, waits for them, and re-layouts  1.87 us (2%)
    pallas_call x1, Pallas kernels, body(): pl.pallas_call(functools.partial(kernel, (ctx_count, tokens, block, width...  95.9 us

profile of v6, /device:TPU:0, one launch (start us, length us, event | category | flops | bytes accessed | tf_op | source)
XLA Modules:
  0.0 97.7 jit_solution(16603143253511950162)
XLA Ops:
  0.0 95.9 %shard_map.100 = bf16[512,512]{1,0:T(8,128)(2,1)} custom-call(s32[8]{0:T(128)} %live_ref.1, s32[3]{0:T(128)} %lengths_ref.1, f32[1,8192]{1,0:T(1,128)} %bitcast.2, f32[3,3,256]{2,1,0:T(4,128)} %taps_hbm.1, f32[16,256]{1,0:T(8,128)} %rates_hbm.1, f32[16,256]{1,0:T(8,128)} %residues_hbm.1, f32[1,256]{1,0:T(1,128)} %bitcast.3, bf16[1024,512]{1,0:T(8,128)(2,1)} %x_hbm.1, ...), custom_call_target="tpu_custom_call" | custom-call | flops 8589934592 | bytes 18874368 | tf_op jit(solution)/shard_map/pallas_call | solution.py:649
  95.9 1.9 %copy.12 = bf16[512,512]{1,0:T(8,128)(2,1)} copy(bf16[512,512]{1,0:T(8,128)(2,1)} %shard_map.100) | data formatting | bytes 1048576

commit v7 on v5

--- a/solution.py
+++ b/solution.py
@@ -589,8 +589,7 @@
         to_partner(0).wait_recv()
 
     rest_g(last_leg, lambda: None)
-    for h in range(2):
-        out_ref[:, pl.ds(h * half, half)] = jnp.transpose(out_sum[pl.ds(h * half, half), :]).astype(jnp.bfloat16)
+    out_ref[...] = out_sum[...].astype(jnp.bfloat16)
 
     to_next.wait_send()
     to_previous.wait_send()
@@ -638,9 +637,9 @@
     anywhere = pl.BlockSpec(memory_space=pl.ANY)
     dma = pltpu.SemaphoreType.DMA
     flops = 2 * tokens * width * BRANCHES * channels + 2 * tokens * features * ch_count * channels
-    return pl.pallas_call(
+    by_token = pl.pallas_call(
         functools.partial(kernel, (ctx_count, tokens, block, width)),
-        out_shape=jax.ShapeDtypeStruct((features, tokens), bf16),
+        out_shape=jax.ShapeDtypeStruct((tokens, features), bf16),
         in_specs=[smem, smem] + [anywhere] * 8,
         out_specs=vmem,
         scratch_shapes=[
@@ -695,6 +694,7 @@
         w_in,
         w_out,
     )
+    return by_token.T
 
 
 def solution(mesh):

time: 97.8 us -> 97.8 us (level)
    transpose x0 -> x1, local copies, waits for them, and re-layouts: none -> 2.05 us  [body(): return by_token.T]
    unnamed x1 -> x0, local copies, waits for them, and re-layouts: 1.87 us -> none
where the time goes in v7:
time: 97.8 us; the launch traced here: 97.6 us
  Pallas kernels  95.6 us (98%)
  local copies, waits for them, and re-layouts  2.05 us (2%)
    pallas_call x1, Pallas kernels, body(): pl.pallas_call(functools.partial(kernel, (ctx_count, tokens, block, width...  95.6 us
    transpose x1, local copies, waits for them, and re-layouts, body(): return by_token.T  2.05 us

profile of v7, /device:TPU:0, one launch (start us, length us, event | category | flops | bytes accessed | tf_op | source)
XLA Modules:
  0.0 97.6 jit_solution(11883515544038419479)
XLA Ops:
  0.0 95.6 %shard_map.100 = bf16[512,512]{1,0:T(8,128)(2,1)} custom-call(s32[8]{0:T(128)} %live_ref.1, s32[3]{0:T(128)} %lengths_ref.1, f32[1,8192]{1,0:T(1,128)} %bitcast.4, f32[3,3,256]{2,1,0:T(4,128)} %taps_hbm.1, f32[16,256]{1,0:T(8,128)} %rates_hbm.1, f32[16,256]{1,0:T(8,128)} %residues_hbm.1, f32[1,256]{1,0:T(1,128)} %bitcast.5, bf16[1024,512]{1,0:T(8,128)(2,1)} %x_hbm.1, ...), custom_call_target="tpu_custom_call" | custom-call | flops 8589934592 | bytes 18874368 | tf_op jit(solution)/shard_map/pallas_call | solution.py:640
  95.6 2.0 %copy.11 = bf16[512,512]{1,0:T(8,128)(2,1)} copy(bf16[512,512]{0,1:T(8,128)(2,1)} %bitcast.3) | data formatting | bytes 1048576 | tf_op jit(solution)/shard_map/transpose | solution.py:697
